TPU v7x, 256 devices: a whole 4x4x8 slice. The times are simulated.
256 devices in a mesh: space: 128 (over z, y, x_hi, core), blk: 2 (over x_lo).
Axes of the slice: x: 4 (x_hi: 2, x_lo: 2; x = x_hi * 2 + x_lo), y: 4, z: 8, core: 2. Of those that a mesh axis runs over, the one named last changes fastest.
Arguments:
- record: bfloat16 [32, 128, 196608], P('blk', None, 'space'), may hold values from -10 to 10, as said below
- weights: float32 [196608], P('space'), may hold values from 0.0625 to 9
Outputs:
- modes: bfloat16 [64, 2, 32, 196608], P('blk', None, None, 'space')
- energies: float32 [64, 64], P('blk')
Inputs may be any that keep to these rules, and one draw needn't show every extreme that they name: `record`: the snapshots of all blocks share a common part.
All inputs are finite; a program needn't handle non-finite values.
Results may differ from a plain program's by a relative error of at most 0.0073.
Values may be sent and summed in bfloat16 or wider, within the bound.
No kernel may reach another device: no remote copies, remote signals or barrier semaphores. Data moves between devices by JAX's collectives and lax.ppermute only.
A program may use at most 128 MiB of HBM per device.

v0:
```python
import math

import jax
import jax.numpy as jnp
from jax import lax
from jax.sharding import PartitionSpec as P

NF = 64


def spectral_table(freq_count, time_steps):
    time_index = jnp.arange(time_steps, dtype=jnp.int32)
    freq_index = jnp.arange(freq_count, dtype=jnp.int32)
    phases = (freq_index[:, None] * time_index[None, :] % time_steps).astype(jnp.float32) * (
        2.0 * math.pi / time_steps
    )
    window = 0.5 - 0.5 * jnp.cos(time_index.astype(jnp.float32) * (2.0 * math.pi / time_steps))
    window_norm = jnp.sqrt(jnp.sum(window * window))
    rows_cos = window * jnp.cos(phases) / window_norm
    rows_sin = -window * jnp.sin(phases) / window_norm
    return jnp.stack([rows_cos, rows_sin], axis=1).astype(jnp.bfloat16)


def local(record, weights):
    blocks_here, time_steps, points = record.shape
    owners = lax.axis_size("blk")
    local_freqs = NF // owners
    spectral_rows = spectral_table(NF, time_steps).reshape(NF * 2, time_steps)
    spectra = jnp.dot(spectral_rows, record, preferred_element_type=jnp.float32).astype(
        jnp.bfloat16
    )
    spectra = spectra.reshape(owners, local_freqs, 2, blocks_here, points)
    gathered = lax.all_to_all(spectra, "blk", split_axis=0, concat_axis=3, tiled=True)[0]
    weighted = (gathered.astype(jnp.float32) * weights).astype(jnp.bfloat16)
    partial_value = jnp.einsum(
        "fcip,fdjp->fcidj", gathered, weighted, preferred_element_type=jnp.float32
    )
    real_part = partial_value[:, 0, :, 0, :] + partial_value[:, 1, :, 1, :]
    imag_part = partial_value[:, 0, :, 1, :] - partial_value[:, 1, :, 0, :]
    blocks = real_part.shape[-1]
    real_part, imag_part = lax.psum((real_part, imag_part), "space")
    point_count = points * lax.axis_size("space")
    real_part = real_part / point_count
    imag_part = imag_part / point_count
    embedded = jnp.concatenate(
        [
            jnp.concatenate([real_part, -imag_part], axis=-1),
            jnp.concatenate([imag_part, real_part], axis=-1),
        ],
        axis=-2,
    )
    factor = jnp.linalg.cholesky(embedded)
    energies = jnp.diagonal(factor, axis1=-2, axis2=-1) ** 2
    first = jnp.concatenate([gathered[:, 0], -gathered[:, 1]], axis=1)
    second = jnp.concatenate([gathered[:, 1], gathered[:, 0]], axis=1)
    stacked = jnp.stack([first, second], axis=1)
    factors = jnp.broadcast_to(factor[:, None], (factor.shape[0], 2) + factor.shape[1:])
    solved = lax.linalg.triangular_solve(
        factors, stacked.astype(jnp.float32), left_side=True, lower=True
    )
    modes = solved[:, :, blocks:, :].astype(jnp.bfloat16)
    return (modes, energies)


def solution(mesh):
    return jax.shard_map(
        local,
        mesh=mesh,
        in_specs=(P("blk", None, "space"), P("space")),
        out_specs=(P("blk", None, None, "space"), P("blk", None)),
        check_vma=False,
    )
```

profile of v0, /device:TPU:1, one launch (start us, length us, event | category | flops | bytes accessed | tf_op | source)
XLA Modules:
  0.0 1782.5 jit_solution(17753693707623668712)
XLA Ops:
  7.2 0.6 multiply_reduce_fusion
  8.6 0.2 divide_convert_fusion
  8.8 7.3 convolution_convert_fusion
  16.1 13.1 reshape.152
  29.2 6.8 copy.56
  36.0 6.3 all-to-all-start
  42.3 0.2 all-reduce.3.cloned.1.call-start
  42.6 67.6 %all-to-all-done = bf16[2,32,2,16,1536]{4,2,1,3,0:T(2,128)(2,1)} async-done(((bf16[2,32,2,16,1536]{4,2,1,3,0:T(2,128)(2,1)}), bf16[2,32,2,16,1536]{4,2,1,3,0:T(2,128)(2,1)}, u32[]{:S(2)}, u32[]{:S(2)}) %all-to-all-start) | async-done | bytes 6291488 | tf_op jit(solution)/shard_map/all_to_all | solution.py:33
  110.2 9.0 copy.72
  119.2 7.9 copy.57
  127.1 0.0 copy-start
  127.1 0.2 fusion.16
  127.3 1.9 slice_bitcast_fusion
  129.2 0.0 copy-done
  129.2 9.6 fusion.3
  138.8 2.7 fusion.6
  141.5 3.9 slice_bitcast_fusion.1
  145.4 0.0 all-reduce.3.cloned.1.call-update
  145.5 9.4 maximum_bitcast_fusion
  154.9 1260.3 %all-reduce.3.cloned.1.call-done = (f32[32,32,32]{1,2,0:T(8,128)}, f32[32,32,32]{1,2,0:T(8,128)}) async-done(((f32[32,32,32]{1,2,0:T(8,128)}, f32[32,32,32]{1,2,0:T(8,128)}), (f32[32,32,32]{1,2,0:T(8,128)}, f32[32,32,32]{1,2,0:T(8,128)})) %all-reduce.3.cloned.1.call-update) | async-done | bytes 262160 | tf_op jit(solution)/shard_map/psum | solution.py:41
  1415.1 1.1 broadcast_multiply_fusion.1
  1416.2 1.2 fusion.15
  1417.4 1.3 maximum_maximum_fusion
  1418.7 1.6 copy.62
  1420.3 1.3 fusion.5
  1421.6 188.2 %custom-call.7 = f32[32,64,64]{2,1,0:T(8,128)S(1)} custom-call(f32[32,64,64]{2,1,0:T(8,128)} %fusion.5), custom_call_target="Cholesky" | custom-call | tf_op jit(solution)/shard_map/jit(cholesky)/cholesky | solution.py:52
  1609.9 0.1 select_reduce_fusion
  1610.0 0.1 compare_reduce_fusion
  1610.1 0.2 select_select_fusion
  1610.3 0.7 copy.63
  1611.0 2.9 broadcast_select_fusion
  1613.9 0.9 gather_fusion
  1614.7 0.7 copy.68
  1615.4 134.0 %custom-call.8 = f32[32,2,1,64,64]{0,3,4,2,1:T(8,128)} custom-call(f32[32,2,1,64,64]{0,4,3,2,1:T(8,128)} %broadcast_select_fusion), custom_call_target="InvertDiagBlocksLowerTriangular" | custom-call | tf_op jit(solution)/shard_map/triangular_solve | solution.py:58
  1749.4 4.4 copy.65
  1753.8 15.6 fusion
  1769.4 6.2 slice.63
  (8 shorter events, 0.2 us)
Async XLA Ops:
  36.0 74.2 %all-to-all-start = ((bf16[2,32,2,16,1536]{4,2,1,3,0:T(2,128)(2,1)}), bf16[2,32,2,16,1536]{4,2,1,3,0:T(2,128)(2,1)}, u32[]{:S(2)}, u32[]{:S(2)}) async-start(bf16[2,32,2,16,1536]{4,2,1,3,0:T(2,128)(2,1)} %copy.56), calls=%async_computation | async-start | bytes 12582912 | tf_op jit(solution)/shard_map/all_to_all | solution.py:33
  42.3 1372.8 %all-reduce.3.cloned.1.call-start = ((), (), s32[]{:S(2)}) async-start(), calls=%async_computation.1 | async-start | bytes 2097152 | tf_op jit(solution)/shard_map/psum | solution.py:41
  127.1 2.1 copy-start
Sparse Core Ops, SparseCore 0:
  145.6 1269.5 all-reduce.2
where the time goes:
time: 1790 us; the launch traced here: 1780 us
  waiting for transfers between devices  1330 us (74%)
  other arithmetic  344 us (19%)
  local copies, waits for them, and re-layouts  57 us (3%)
  matrix products  32.5 us (2%)
    psum x1, waiting for transfers between devices, local(): real_part, imag_part = lax.psum((real_part, imag_part), 'space')  1260 us
    another operation x4, other arithmetic, local(): factor = jnp.linalg.cholesky(embedded)  188 us
    another operation x3, other arithmetic, local(): lax.linalg.triangular_solve(factors, stacked.astype(jnp.float32), left_si...  137 us
    all_to_all x1, waiting for transfers between devices, local(): lax.all_to_all(spectra, 'blk', split_axis=0, concat_axis=3, tiled=True)[0]  67.6 us
  transfers between devices with their start and end apart: 2, of which 2 were waited for; matrix products, arithmetic and copies ran while one was open for 1% of the time, Pallas kernels for 0%

commit v1 on v0

v1 whole, which is shorter than its diff:
```python
import functools
import math

import jax
import jax.numpy as jnp
import numpy as np
from jax import lax
from jax.experimental import pallas as pl
from jax.experimental.pallas import tpu as pltpu
from jax.sharding import Mesh
from jax.sharding import PartitionSpec as P

NF = 64
NT = 128
GROUPS = (1, 1, 2)
FINE = ("z", "y", "xh", "core", "blk")
AHEAD = 3
MIB = 1024 * 1024


def spectral_table():
    time_index = np.arange(NT, dtype=np.int32)
    freq_index = np.arange(NF, dtype=np.int32)
    step = np.float32(2.0 * math.pi / NT)
    phases = (freq_index[:, None] * time_index[None, :] % NT).astype(np.float32) * step
    window = np.float32(0.5) - np.float32(0.5) * np.cos(time_index.astype(np.float32) * step)
    norm = np.sqrt(np.sum(window * window))
    rows_cos = window * np.cos(phases) / norm
    rows_sin = -window * np.sin(phases) / norm
    return np.stack([rows_cos, rows_sin], axis=1).astype(jnp.bfloat16)


def pair_table(first_owner):
    table = spectral_table().reshape(2, 4, 8, 2, NT)
    out = np.zeros((2, 4, 2, 2, 8, 2, NT), dtype=table.dtype)
    for b in range(2):
        out[:, :, :, b, :, b, :] = table.transpose(0, 1, 3, 2, 4)
    if first_owner:
        out = out[::-1]
    return np.ascontiguousarray(out).reshape(256, 256)


def early_kernel(first, owner_ref, tables_ref, record_ref, out_ref, table, rows, table_sem, sems):
    pairs, _, _, points = rows.shape
    head = pltpu.make_async_copy(tables_ref.at[owner_ref[0]], table, table_sem)
    head.start()
    copies = [
        pltpu.make_async_copy(
            record_ref.at[pl.ds(2 * (first + p), 2)], rows.at[p], sems.at[p]
        )
        for p in range(pairs)
    ]
    for p in range(min(4, pairs)):
        copies[p].start()
    head.wait()
    left = table[...]
    for p in range(pairs):
        copies[p].wait()
        if p + 4 < pairs:
            copies[p + 4].start()
        value = jnp.dot(
            left, rows[p].reshape(256, points), preferred_element_type=jnp.float32
        ).astype(jnp.bfloat16)
        for row in range(0, value.shape[0], 16):
            out_ref[row // 32, row // 16 % 2, p] = value[row : row + 16]


def early_call(owner, tables, record, first, pairs):
    blocks, times, points = record.shape
    count = tables.shape[1] // 32
    out = pl.pallas_call(
        functools.partial(early_kernel, first),
        in_specs=[
            pl.BlockSpec(memory_space=pltpu.SMEM),
            pl.BlockSpec(memory_space=pl.ANY),
            pl.BlockSpec(memory_space=pl.ANY),
        ],
        out_specs=pl.BlockSpec(memory_space=pltpu.VMEM),
        out_shape=jax.ShapeDtypeStruct((count, 2, pairs, 16, points), jnp.bfloat16),
        scratch_shapes=[
            pltpu.VMEM((32 * count, 256), jnp.bfloat16),
            pltpu.VMEM((pairs, 2, times, points), jnp.bfloat16),
            pltpu.SemaphoreType.DMA,
            pltpu.SemaphoreType.DMA((pairs,)),
        ],
        compiler_params=pltpu.CompilerParams(vmem_limit_bytes=58 * MIB),
        cost_estimate=pl.CostEstimate(
            flops=2 * 32 * count * 256 * points * pairs, bytes_accessed=pairs * MIB, transcendentals=0
        ),
        name="early",
    )(owner, tables, record)
    return out.reshape(count, 2, 16 * pairs, points)


def spectra_kernel(owner_ref, table_ref, record_ref, *outs):
    points = record_ref.shape[-1]
    width = 256
    for start in range(0, points, width):
        cols = pl.ds(start, width)
        rows = record_ref[:, :, cols].reshape(256, width)
        value = jnp.dot(table_ref[0], rows, preferred_element_type=jnp.float32)
        value = value.astype(jnp.bfloat16)
        row = 0
        for out in outs:
            for chunk in range(2):
                for c in range(2):
                    out[chunk, c, 0, :, cols] = value[row : row + 16]
                    row += 16


def spectra_call(owner, tables, record):
    blocks, times, points = record.shape
    pairs = blocks // 2
    count = tables.shape[1] // 32
    outs = pl.pallas_call(
        spectra_kernel,
        grid_spec=pltpu.PrefetchScalarGridSpec(
            num_scalar_prefetch=1,
            grid=(pairs,),
            in_specs=[
                pl.BlockSpec((1, 32 * count, 256), lambda p, owner: (owner[0], 0, 0)),
                pl.BlockSpec((2, times, points), lambda p, owner: (p, 0, 0)),
            ],
            out_specs=[
                pl.BlockSpec((2, 2, 1, 16, points), lambda p, owner: (0, 0, p, 0, 0))
            ]
            * (count // 2),
        ),
        out_shape=[jax.ShapeDtypeStruct((2, 2, pairs, 16, points), jnp.bfloat16)] * (count // 2),
        compiler_params=pltpu.CompilerParams(vmem_limit_bytes=16 * MIB),
        cost_estimate=pl.CostEstimate(
            flops=2 * 32 * count * 256 * points * pairs,
            bytes_accessed=(6 + count) * MIB,
            transcendentals=0,
        ),
        name="spectra",
    )(owner, tables, record)
    return [out.reshape(2, 2, 16 * pairs, points) for out in outs]


def nt_dot(a, b):
    return lax.dot_general(a, b, (((1,), (1,)), ((), ())), preferred_element_type=jnp.float32)


def swap_rows(x):
    half = x.shape[0] // 2
    return jnp.concatenate([x[half:], x[:half]], axis=0)


def swap_lanes(x):
    half = x.shape[1] // 2
    return jnp.concatenate([x[:, half:], x[:, :half]], axis=1)


def upper():
    row = lax.broadcasted_iota(jnp.int32, (32, 256), 0)
    return row >= lax.broadcasted_iota(jnp.int32, (32, 256), 1) // 8


def unpack(packed):
    row_f = lax.broadcasted_iota(jnp.int32, (32, 8, 256), 1)
    same = row_f == lax.broadcasted_iota(jnp.int32, (32, 8, 256), 2) % 8
    spread = jnp.where(same, jnp.broadcast_to(packed[:, None, :], (32, 8, 256)), 0.0)
    turned = spread.reshape(256, 256).T.reshape(32, 8, 256).sum(axis=1)
    row = lax.broadcasted_iota(jnp.int32, (32, 256), 0)
    column = lax.broadcasted_iota(jnp.int32, (32, 256), 1) // 8
    real = jnp.where(row >= column, packed, turned)
    imag = jnp.where(row < column, packed, jnp.where(row > column, -turned, 0.0))
    return real, imag


def gram_kernel(parts, owner_ref, weights_ref, *rest):
    out_ref = rest[-1]
    first = owner_ref[0] == 0
    weights = weights_ref[...]
    row_f = lax.broadcasted_iota(jnp.int32, (256, 256), 0) % 8
    col_f = lax.broadcasted_iota(jnp.int32, (256, 256), 1) % 8
    same = row_f == col_f
    for i in range(out_ref.shape[0]):
        x0, x1 = (jnp.concatenate([ref[i, c] for ref in rest[:parts]], axis=0) for c in range(2))
        w0 = (x0.astype(jnp.float32) * weights).astype(jnp.bfloat16)
        w1 = (x1.astype(jnp.float32) * weights).astype(jnp.bfloat16)
        real = nt_dot(x0, w0) + nt_dot(x1, w1)
        imag = nt_dot(x0, w1) - nt_dot(x1, w0)
        both = []
        for value in (real, imag):
            value = jnp.where(same, value, 0.0).reshape(32, 8, 256).sum(axis=1)
            both.append(jnp.where(first, value, swap_rows(swap_lanes(value))))
        out_ref[i] = jnp.where(upper(), both[0], both[1])


def gram_call(owner, weights, rows):
    chunks, _, _, points = rows[0].shape
    return pl.pallas_call(
        functools.partial(gram_kernel, len(rows)),
        in_specs=[pl.BlockSpec(memory_space=pltpu.SMEM)]
        + [pl.BlockSpec(memory_space=pltpu.VMEM)] * (1 + len(rows)),
        out_specs=pl.BlockSpec(memory_space=pltpu.VMEM),
        out_shape=jax.ShapeDtypeStruct((chunks, 32, 256), jnp.float32),
        compiler_params=pltpu.CompilerParams(vmem_limit_bytes=16 * MIB),
        cost_estimate=pl.CostEstimate(
            flops=8 * 256 * 256 * points * chunks,
            bytes_accessed=2 * MIB * chunks,
            transcendentals=0,
        ),
        name="gram",
    )(owner, weights, *rows)


def eliminate(products, scale):
    lane = lax.broadcasted_iota(jnp.int32, (8, 128), 1)
    lane_f = lane % 8
    lane_row = lane // 8
    sub = lax.broadcasted_iota(jnp.int32, (8, 128), 0)
    states = []
    for real, imag in products:
        real, imag = real * scale, imag * scale
        grid = []
        for q in range(4):
            half = slice(128 * (q % 2), 128 * (q % 2) + 128)
            top, bottom = (real, imag) if q < 2 else (-imag, real)
            grid.append(
                [top[8 * s : 8 * s + 8, half] for s in range(4)]
                + [bottom[8 * s : 8 * s + 8, half] for s in range(4)]
            )
        states.append(grid)
    def column_of(grid, k):
        take = lane_f + 8 * (k % 16)
        return [
            jnp.take_along_axis(grid[k // 16][s], take, axis=1, mode="promise_in_bounds")
            for s in range(8)
        ]

    def row_of(blocks, k):
        return jnp.broadcast_to(blocks[k // 8][k % 8 : k % 8 + 1], (8, 128))

    ahead = [{k: column_of(grid, k) for k in range(AHEAD)} for grid in states]
    for k in range(64):
        q0, group = divmod(k, 16)
        s0, r0 = divmod(k, 8)
        for grid, later in zip(states, ahead):
            column = later.pop(k)
            if k + AHEAD < 64:
                later[k + AHEAD] = column_of(grid, k + AHEAD)
            inverse = 1.0 / row_of(column, k)
            factors = {n: row_of(column, n) * inverse for n in later}
            column[s0] = jnp.where(sub == r0, 1.0, column[s0])
            for n, blocks in later.items():
                blocks[s0] = jnp.where(sub == r0, 0.0, blocks[s0])
                later[n] = [blocks[s] - column[s] * factors[n] for s in range(8)]
            for q in range(q0, 4):
                factor = row_of(grid[q], k) * inverse
                keep = sub != r0
                if q == q0:
                    factor = jnp.where(lane_row > group, factor, 0.0)
                    keep = keep | (lane_row <= group)
                grid[q][s0] = jnp.where(keep, grid[q][s0], 0.0)
                for s in range(8):
                    grid[q][s] = grid[q][s] - column[s] * factor
    return states


def diagonal(grid):
    lane_row = lax.broadcasted_iota(jnp.int32, (8, 128), 1) // 8
    sub = lax.broadcasted_iota(jnp.int32, (8, 128), 0)
    out = []
    for q in range(4):
        total = jnp.zeros((8, 128), jnp.float32)
        for s in (2 * q, 2 * q + 1):
            total = total + jnp.where(lane_row + 16 * q == sub + 8 * s, grid[q][s], 0.0)
        out.append(total.sum(axis=0, keepdims=True))
    return out


def lower_rows(grid, pivots):
    lane_row = lax.broadcasted_iota(jnp.int32, (8, 128), 1) // 8
    sub = lax.broadcasted_iota(jnp.int32, (8, 128), 0)
    halves = []
    for q in (2, 3):
        root = lax.rsqrt(pivots[q])
        blocks = []
        for s in range(8):
            row, column = lane_row + 16 * q, sub + 8 * s
            value = jnp.where(column < row, grid[q][s], jnp.where(column == row, 1.0, 0.0))
            blocks.append(value * root)
        halves.append(jnp.concatenate(blocks, axis=0))
    return jnp.concatenate(halves, axis=1)


def build_maps(scale, owner, sums_ref, energies_ref, maps_ref):
    chunks = sums_ref.shape[0]
    states = eliminate([unpack(sums_ref[i]) for i in range(chunks)], scale)
    out_row = lax.broadcasted_iota(jnp.int32, (256, 256), 0)
    lane = lax.broadcasted_iota(jnp.int32, (256, 256), 1)
    same = out_row // 32 == lane % 8
    order = (same & (out_row % 32 == lane // 8)).astype(jnp.bfloat16)
    b_row = lax.broadcasted_iota(jnp.int32, (32, 256), 0)
    b_lane = lax.broadcasted_iota(jnp.int32, (32, 256), 1) // 8
    spread = (b_row == (b_lane + 16 * owner) % 32).astype(jnp.bfloat16)
    for i, grid in enumerate(states):
        pivots = diagonal(grid)
        for q in range(4):
            energies_ref[i, q : q + 1, :] = pivots[q]
        full = lower_rows(grid, pivots)
        high = full.astype(jnp.bfloat16)
        low = (full - high.astype(jnp.float32)).astype(jnp.bfloat16)
        for level, value in enumerate((high, low)):
            rows = nt_dot(order, value).astype(jnp.bfloat16)
            for c in range(2):
                wide = jnp.dot(
                    rows[:, 32 * c : 32 * c + 32], spread, preferred_element_type=jnp.float32
                )
                wide = jnp.where(same, wide, 0.0)
                at = 256 * (2 * c + level)
                maps_ref[i, 0, :, at : at + 256] = (wide if c == 0 else -wide).astype(jnp.bfloat16)
                at = 256 * (2 * (1 - c) + level)
                maps_ref[i, 1, :, at : at + 256] = wide.astype(jnp.bfloat16)


def apply_maps(maps_ref, i, refs, at, modes_ref, first):
    width = 256
    for start in range(0, refs[0].shape[-1], width):
        cols = pl.ds(start, width)
        x0, x1 = (jnp.concatenate([ref[at, c, :, cols] for ref in refs], axis=0) for c in range(2))
        stacked = jnp.concatenate([x0, x0, x1, x1], axis=0)
        for c in range(2):
            value = jnp.dot(maps_ref[i, c], stacked, preferred_element_type=jnp.float32)
            modes_ref[first : first + 8, c, :, cols] = value.astype(jnp.bfloat16).reshape(
                8, 32, width
            )


def factor_kernel(scale, owner_ref, sums_ref, maps_ref, energies_ref):
    build_maps(scale, owner_ref[0], sums_ref, energies_ref, maps_ref)


def factor_call(owner, sums, point_count):
    chunks = sums.shape[0]
    return pl.pallas_call(
        functools.partial(factor_kernel, 1.0 / point_count),
        in_specs=[
            pl.BlockSpec(memory_space=pltpu.SMEM),
            pl.BlockSpec(memory_space=pltpu.VMEM),
        ],
        out_specs=[pl.BlockSpec(memory_space=pltpu.VMEM)] * 2,
        out_shape=[
            jax.ShapeDtypeStruct((chunks, 2, 256, 1024), jnp.bfloat16),
            jax.ShapeDtypeStruct((chunks, 4, 128), jnp.float32),
        ],
        compiler_params=pltpu.CompilerParams(vmem_limit_bytes=16 * MIB),
        cost_estimate=pl.CostEstimate(
            flops=1 << 30, bytes_accessed=2 * MIB * chunks, transcendentals=0
        ),
        name="factor",
    )(owner, sums)


def apply_kernel(count, maps_ref, *rest):
    apply_maps(maps_ref, 0, rest[:count], 0, rest[-1], 0)


def solve_kernel(scale, parts, owner_ref, sums_ref, *rest):
    modes_ref, energies_ref, maps_ref = rest[-3:]

    @pl.when(pl.program_id(0) == 0)
    def factor():
        build_maps(scale, owner_ref[0], sums_ref, energies_ref, maps_ref)

    for i in range(sums_ref.shape[0]):
        apply_maps(maps_ref, i, rest[:parts], i, modes_ref, 8 * i)


def row_specs(rows, tiles, chunks, first):
    return [
        pl.BlockSpec(
            (chunks, *part.shape[1:3], part.shape[3] // tiles), lambda t: (first, 0, 0, t)
        )
        for part in rows
    ]


def modes_shape(total_chunks, points):
    return jax.ShapeDtypeStruct((8 * total_chunks, 2, 32, points), jnp.bfloat16)


def apply_call(maps, index, rows, modes, base, total_chunks, tiles=2):
    points = rows[0].shape[-1]
    operands = [maps, *rows]
    in_specs = [pl.BlockSpec((1, 2, 256, 1024), lambda t: (index, 0, 0, 0))]
    in_specs += row_specs(rows, tiles, 1, index)
    aliases = {}
    if modes is not None:
        aliases = {len(operands): 0}
        in_specs.append(pl.BlockSpec(memory_space=pl.ANY))
        operands.append(modes)
    return pl.pallas_call(
        functools.partial(apply_kernel, len(rows)),
        grid=(tiles,),
        in_specs=in_specs,
        out_specs=pl.BlockSpec((8, 2, 32, points // tiles), lambda t: (base, 0, 0, t)),
        out_shape=modes_shape(total_chunks, points),
        input_output_aliases=aliases,
        compiler_params=pltpu.CompilerParams(vmem_limit_bytes=16 * MIB),
        cost_estimate=pl.CostEstimate(
            flops=16 * 256 * 256 * points, bytes_accessed=4 * MIB, transcendentals=0
        ),
        name="apply",
    )(*operands)


def solve_call(owner, sums, rows, modes, base, total_chunks, point_count, tiles=2):
    chunks, _, _, points = rows[0].shape
    return pl.pallas_call(
        functools.partial(solve_kernel, 1.0 / point_count, len(rows)),
        grid=(tiles,),
        in_specs=[
            pl.BlockSpec(memory_space=pltpu.SMEM),
            pl.BlockSpec((chunks, 32, 256), lambda t: (0, 0, 0)),
            *row_specs(rows, tiles, chunks, 0),
            pl.BlockSpec(memory_space=pl.ANY),
        ],
        out_specs=[
            pl.BlockSpec(
                (8 * chunks, 2, 32, points // tiles), lambda t: (base // chunks, 0, 0, t)
            ),
            pl.BlockSpec((chunks, 4, 128), lambda t: (0, 0, 0)),
        ],
        out_shape=[
            modes_shape(total_chunks, points),
            jax.ShapeDtypeStruct((chunks, 4, 128), jnp.float32),
        ],
        scratch_shapes=[pltpu.VMEM((chunks, 2, 256, 1024), jnp.bfloat16)],
        input_output_aliases={2 + len(rows): 0},
        compiler_params=pltpu.CompilerParams(vmem_limit_bytes=20 * MIB),
        cost_estimate=pl.CostEstimate(
            flops=16 * 256 * 256 * points * chunks,
            bytes_accessed=chunks * 4 * MIB,
            transcendentals=0,
        ),
        name="solve",
    )(owner, sums, *rows, modes)


def after(value, *others):
    return lax.optimization_barrier((value, *others))[0]


def involution(pairs):
    return pairs + [(b, a) for a, b in pairs]


STEPS = (
    ("core", involution([(0, 1)])),
    ("y", involution([(0, 1), (2, 3)])),
    ("y", involution([(0, 3), (1, 2)])),
    ("z", involution([(0, 1), (2, 3), (4, 5), (6, 7)])),
    ("z", involution([(0, 5), (1, 4), (2, 7), (3, 6)])),
    ("z", involution([(1, 2), (3, 4), (5, 6), (7, 0)])),
    ("xh", involution([(0, 1)])),
)
ROUND = (("z", "xh"), involution([(2 * z, 2 * (z ^ 1) + 1) for z in range(8)]))


def add_step(value, step):
    axis, pairs = step
    return value + lax.ppermute(value, axis, pairs)


def local(record, weights):
    points = record.shape[-1]
    space = 1
    for axis in FINE[:-1]:
        space *= lax.axis_size(axis)
    owner = lax.axis_index("blk").astype(jnp.int32).reshape(1)
    wide = weights.reshape(1, points)
    tables = np.stack([pair_table(0), pair_table(1)])
    part = lambda a, b: jnp.asarray(tables[:, a:b])
    swap = lambda s: lax.ppermute(s, "blk", [(0, 1), (1, 0)])
    gram = functools.partial(gram_call, owner, wide)
    solve = functools.partial(solve_call, owner, total_chunks=4, point_count=points * space)

    away_a = early_call(owner, part(128, 192), record, 0, 2)
    peer_a = swap(away_a)
    away_b = early_call(owner, part(128, 192), after(record, away_a), 2, 6)
    peer_b = swap(away_b)
    rest = np.concatenate([tables[:, 192:], tables[:, :128]], axis=1)
    away_cd, own_ab, own_cd = spectra_call(
        owner, jnp.asarray(rest), after(record, peer_a, away_b)
    )
    rows_ab = [own_ab, peer_a, peer_b]
    rows_cd = [own_cd, swap(away_cd)]

    ab = gram(rows_ab)
    for step in STEPS[:6] + (ROUND,):
        ab = add_step(ab, step)
    cd = gram(lax.optimization_barrier((*rows_cd, ab))[:2])
    for step in STEPS[:3]:
        cd = add_step(cd, step)
    maps, pivots_ab = factor_call(owner, after(ab, cd), points * space)
    for step in STEPS[3:5]:
        cd = add_step(cd, step)
    maps = after(maps, cd)
    modes = apply_call(maps, 0, rows_ab, None, 0, 4)
    cd = add_step(after(cd, maps), STEPS[5])
    modes = apply_call(after(maps, cd), 1, rows_ab, modes, 1, 4)
    cd = add_step(cd, STEPS[6])
    modes, pivots_cd = solve(cd, rows_cd, modes, 2)
    pivots = jnp.concatenate([pivots_ab, pivots_cd], axis=0)
    energies = pivots.reshape(-1, 64, 8).transpose(0, 2, 1).reshape(-1, 64)
    return (modes, energies)


def solution(mesh):
    fine = Mesh(mesh.devices.reshape(8, 4, 2, 2, 2), FINE)
    return jax.shard_map(
        local,
        mesh=fine,
        in_specs=(P("blk", None, FINE[:-1]), P(FINE[:-1])),
        out_specs=(P("blk", None, None, FINE[:-1]), P("blk", None)),
        check_vma=False,
    )
```

time: 1790 us -> 130 us (0.07)
  the two profiles are of different devices: /device:TPU:1 before, /device:TPU:24 now
where the time goes in v1:
time: 130 us
  waiting for transfers between devices  61.7 us (47%)
  Pallas kernels  32 us (25%)
  starting transfers between devices  31.3 us (24%)
  local copies, waits for them, and re-layouts  3.6 us (3%)
    ppermute x14, waiting for transfers between devices, add_step(): return value + lax.ppermute(value, axis, pairs)  38 us
    ppermute x14, starting transfers between devices, add_step(): return value + lax.ppermute(value, axis, pairs)  27.5 us
    ppermute x3, waiting for transfers between devices, local(): swap = lambda s: lax.ppermute(s, 'blk', [(0, 1), (1, 0)])  23.8 us
    pallas_call x1, Pallas kernels, solve_call(): pl.pallas_call(functools.partial(solve_kernel, 1.0 / point_count, len(row...  8.64 us
    pallas_call x2, Pallas kernels, early_call(): pl.pallas_call(functools.partial(early_kernel, first), in_specs=[pl.Block...  6.73 us
    pallas_call x2, Pallas kernels, apply_call(): pl.pallas_call(functools.partial(apply_kernel, len(rows)), grid=(tiles,),...  5.98 us
    pallas_call x2, Pallas kernels, gram_call(): pl.pallas_call(functools.partial(gram_kernel, len(rows)), in_specs=[pl.Bl...  4.11 us
    ppermute x3, starting transfers between devices, local(): swap = lambda s: lax.ppermute(s, 'blk', [(0, 1), (1, 0)])  3.78 us
  transfers between devices with their start and end apart: 17, of which 14 were waited for; matrix products, arithmetic and copies ran while one was open for 0% of the time, Pallas kernels for 15%

profile of v1, /device:TPU:24, one launch (start us, length us, event | category | flops | bytes accessed | tf_op | source)
XLA Modules:
  0.0 129.6 jit_solution(6392253712631342520)
XLA Ops:
  0.6 2.4 %early.2 = bf16[2,2,2,16,1536]{4,3,2,1,0:T(8,128)(2,1)} custom-call(s32[1]{0:T(128)} %bitcast.owner_ref, bf16[2,64,256]{2,1,0:T(8,128)(2,1)} %constant.8.clone.tables_ref, bf16[16,128,1536]{2,1,0:T(8,128)(2,1)} %record_ref.3), custom_call_target="tpu_custom_call" | custom-call | flops 100663296 | bytes 2097152 | tf_op jit(solution)/shard_map/early/pallas_call | solution.py:71
  3.1 0.0 copy-start.1
  3.1 1.6 %collective-permute-start = (bf16[2,2,32,1536]{3,2,1,0:T(8,128)(2,1)}, bf16[2,2,32,1536]{3,2,1,0:T(8,128)(2,1)S(1)}, u32[]{:S(2)}, u32[]{:S(2)}) collective-permute-start(bf16[2,2,32,1536]{3,2,1,0:T(8,128)(2,1)} %bitcast.16), channel_id=1, source_target_pairs={{0,1},{1,0},{2,3},{3,2},{4,5},{5,4},{6,7},{7,6},{8,9},{9,8},{10,11... | collective-permute-start | bytes 1179656 | tf_op jit(solution)/shard_map/ppermute | solution.py:478
  4.7 4.3 %early.3 = bf16[2,2,6,16,1536]{4,3,2,1,0:T(8,128)(2,1)} custom-call(s32[1]{0:T(128)} %bitcast.owner_ref, bf16[2,64,256]{2,1,0:T(8,128)(2,1)} %constant.8.clone.tables_ref, bf16[16,128,1536]{2,1,0:T(8,128)(2,1)} %record_ref.3), custom_call_target="tpu_custom_call" | custom-call | flops 301989888 | bytes 6291456 | tf_op jit(solution)/shard_map/early/pallas_call | solution.py:71
  9.0 0.6 collective-permute-start.2
  9.6 5.8 %collective-permute-done.rest_1_ = bf16[2,2,32,1536]{3,2,1,0:T(8,128)(2,1)S(1)} collective-permute-done((bf16[2,2,32,1536]{3,2,1,0:T(8,128)(2,1)}, bf16[2,2,32,1536]{3,2,1,0:T(8,128)(2,1)S(1)}, u32[]{:S(2)}, u32[]{:S(2)}) %collective-permute-start) | collective-permute-done | bytes 393248 | tf_op jit(solution)/shard_map/ppermute | solution.py:478
  15.4 0.0 copy-done.1
  15.4 0.0 copy-start
  15.4 2.8 %copy-done = bf16[16,128,1536]{2,1,0:T(8,128)(2,1)S(1)} copy-done((bf16[16,128,1536]{2,1,0:T(8,128)(2,1)S(1)}, bf16[16,128,1536]{2,1,0:T(8,128)(2,1)}, u32[]{:S(2)}) %copy-start) | copy-done | bytes 6291480
  18.2 0.0 copy-start.2
  18.2 2.9 %spectra.1 = (bf16[2,2,8,16,1536]{4,3,2,1,0:T(8,128)(2,1)S(1)}, bf16[2,2,8,16,1536]{4,3,2,1,0:T(8,128)(2,1)S(1)}, bf16[2,2,8,16,1536]{4,3,2,1,0:T(8,128)(2,1)S(1)}) custom-call(s32[1]{0:T(128)} %bitcast.owner_ref, bf16[2,192,256]{2,1,0:T(8,128)(2,1)S(1)} %copy-done.1, bf16[16,128,1536]{2,1,0:T(8,128)(2,1)S(1)} %copy-done), custom_call_target="tpu_custom_call" | custom-call | flops 1207959552 | bytes 12582912 | tf_op jit(solution)/shard_map/spectra/pallas_call | solution.py:115
  21.1 1.6 %collective-permute-start.1 = (bf16[2,2,128,1536]{3,2,1,0:T(8,128)(2,1)S(1)}, bf16[2,2,128,1536]{3,2,1,0:T(8,128)(2,1)S(1)}, u32[]{:S(2)}, u32[]{:S(2)}) collective-permute-start(bf16[2,2,128,1536]{3,2,1,0:T(8,128)(2,1)S(1)} %bitcast.13), channel_id=1, source_target_pairs={{0,1},{1,0},{2,3},{3,2},{4,5},{5,4},{6,7},{7,6},{8,9},{9,8},{10,11... | collective-permute-start | bytes 4718600 | tf_op jit(solution)/shard_map/ppermute | solution.py:478
  22.7 0.0 copy-done.2
  22.7 18.0 %collective-permute-done.2.rest_2_ = bf16[2,2,96,1536]{3,2,1,0:T(8,128)(2,1)S(1)} collective-permute-done((bf16[2,2,96,1536]{3,2,1,0:T(8,128)(2,1)}, bf16[2,2,96,1536]{3,2,1,0:T(8,128)(2,1)S(1)}, u32[]{:S(2)}, u32[]{:S(2)}) %collective-permute-start.2) | collective-permute-done | bytes 1179680 | tf_op jit(solution)/shard_map/ppermute | solution.py:478
  40.7 2.1 %gram.2 = f32[2,32,256]{2,1,0:T(8,128)S(1)} custom-call(s32[1]{0:T(128)} %bitcast.owner_ref, f32[1,1536]{1,0:T(1,128)S(1)} %reshape.32.weights_ref, bf16[2,2,128,1536]{3,2,1,0:T(8,128)(2,1)S(1)} %bitcast.8, bf16[2,2,32,1536]{3,2,1,0:T(8,128)(2,1)S(1)} %collective-permute-done.rest_1_, bf16[2,2,96,1536]{3,2,1,0:T(8,128)(2,1)S(1)} %collective-permute-done.2.rest_2_), custom_call_target="tpu_custom_call" | custom-call | flops 1610612736 | bytes 4194304 | tf_op jit(solution)/shard_map/gram/pallas_call | solution.py:194
  42.7 0.1 collective-permute-start.3
  42.8 1.2 collective-permute-done.3
  44.1 0.8 collective-permute-start.4
  44.9 3.5 %collective-permute-done.4 = f32[2,32,256]{2,1,0:T(8,128)S(1)} collective-permute-done((f32[2,32,256]{2,1,0:T(8,128)S(1)}, f32[2,32,256]{2,1,0:T(8,128)S(1)}, u32[]{:S(2)}, u32[]{:S(2)}) %collective-permute-start.4) | collective-permute-done | bytes 65568 | tf_op jit(solution)/shard_map/ppermute | solution.py:466
  48.5 1.4 %collective-permute-start.5 = (f32[2,32,256]{2,1,0:T(8,128)S(1)}, f32[2,32,256]{2,1,0:T(8,128)S(1)}, u32[]{:S(2)}, u32[]{:S(2)}) collective-permute-start(f32[2,32,256]{2,1,0:T(8,128)S(1)} %add.43), channel_id=1, source_target_pairs={{0,24},{8,16},{24,0},{16,8},{1,25},{9,17},{25,1},{17,9},{2,26},{10... | collective-permute-start | bytes 196616 | tf_op jit(solution)/shard_map/ppermute | solution.py:466
  49.9 4.2 %collective-permute-done.5 = f32[2,32,256]{2,1,0:T(8,128)S(1)} collective-permute-done((f32[2,32,256]{2,1,0:T(8,128)S(1)}, f32[2,32,256]{2,1,0:T(8,128)S(1)}, u32[]{:S(2)}, u32[]{:S(2)}) %collective-permute-start.5) | collective-permute-done | bytes 65568 | tf_op jit(solution)/shard_map/ppermute | solution.py:466
  54.0 2.0 %collective-permute-start.6 = (f32[2,32,256]{2,1,0:T(8,128)S(1)}, f32[2,32,256]{2,1,0:T(8,128)S(1)}, u32[]{:S(2)}, u32[]{:S(2)}) collective-permute-start(f32[2,32,256]{2,1,0:T(8,128)S(1)} %add.44), channel_id=1, source_target_pairs={{0,32},{64,96},{128,160},{192,224},{32,0},{96,64},{160,128},{224,1... | collective-permute-start | bytes 196616 | tf_op jit(solution)/shard_map/ppermute | solution.py:466
  56.0 2.4 %collective-permute-done.6 = f32[2,32,256]{2,1,0:T(8,128)S(1)} collective-permute-done((f32[2,32,256]{2,1,0:T(8,128)S(1)}, f32[2,32,256]{2,1,0:T(8,128)S(1)}, u32[]{:S(2)}, u32[]{:S(2)}) %collective-permute-start.6) | collective-permute-done | bytes 65568 | tf_op jit(solution)/shard_map/ppermute | solution.py:466
  58.4 6.8 %collective-permute-start.7 = (f32[2,32,256]{2,1,0:T(8,128)S(1)}, f32[2,32,256]{2,1,0:T(8,128)S(1)}, u32[]{:S(2)}, u32[]{:S(2)}) collective-permute-start(f32[2,32,256]{2,1,0:T(8,128)S(1)} %add.45), channel_id=1, source_target_pairs={{0,160},{32,128},{64,224},{96,192},{160,0},{128,32},{224,64},{192,... | collective-permute-start | bytes 196616 | tf_op jit(solution)/shard_map/ppermute | solution.py:466
  65.2 2.9 %collective-permute-done.7 = f32[2,32,256]{2,1,0:T(8,128)S(1)} collective-permute-done((f32[2,32,256]{2,1,0:T(8,128)S(1)}, f32[2,32,256]{2,1,0:T(8,128)S(1)}, u32[]{:S(2)}, u32[]{:S(2)}) %collective-permute-start.7) | collective-permute-done | bytes 65568 | tf_op jit(solution)/shard_map/ppermute | solution.py:466
  68.2 4.3 %collective-permute-start.8 = (f32[2,32,256]{2,1,0:T(8,128)S(1)}, f32[2,32,256]{2,1,0:T(8,128)S(1)}, u32[]{:S(2)}, u32[]{:S(2)}) collective-permute-start(f32[2,32,256]{2,1,0:T(8,128)S(1)} %add.46), channel_id=1, source_target_pairs={{32,64},{96,128},{160,192},{224,0},{64,32},{128,96},{192,160},{0,2... | collective-permute-start | bytes 196616 | tf_op jit(solution)/shard_map/ppermute | solution.py:466
  72.5 2.2 %collective-permute-done.8 = f32[2,32,256]{2,1,0:T(8,128)S(1)} collective-permute-done((f32[2,32,256]{2,1,0:T(8,128)S(1)}, f32[2,32,256]{2,1,0:T(8,128)S(1)}, u32[]{:S(2)}, u32[]{:S(2)}) %collective-permute-start.8) | collective-permute-done | bytes 65568 | tf_op jit(solution)/shard_map/ppermute | solution.py:466
  74.7 0.9 collective-permute-start.9
  75.7 5.8 %collective-permute-done.9 = f32[2,32,256]{2,1,0:T(8,128)S(1)} collective-permute-done((f32[2,32,256]{2,1,0:T(8,128)S(1)}, f32[2,32,256]{2,1,0:T(8,128)S(1)}, u32[]{:S(2)}, u32[]{:S(2)}) %collective-permute-start.9) | collective-permute-done | bytes 65568 | tf_op jit(solution)/shard_map/ppermute | solution.py:466
  81.5 0.0 collective-permute-done.1.rest_1_
  81.5 2.1 %gram.3 = f32[2,32,256]{2,1,0:T(8,128)S(1)} custom-call(s32[1]{0:T(128)} %bitcast.owner_ref, f32[1,1536]{1,0:T(1,128)S(1)} %reshape.32.weights_ref, bf16[2,2,128,1536]{3,2,1,0:T(8,128)(2,1)S(1)} %bitcast.11, bf16[2,2,128,1536]{3,2,1,0:T(8,128)(2,1)S(1)} %collective-permute-done.1.rest_1_), custom_call_target="tpu_custom_call" | custom-call | flops 1610612736 | bytes 4194304 | tf_op jit(solution)/shard_map/gram/pallas_call | solution.py:194
  83.6 0.1 collective-permute-start.10
  83.7 1.2 collective-permute-done.10
  84.9 0.1 collective-permute-start.11
  85.0 4.3 %collective-permute-done.11 = f32[2,32,256]{2,1,0:T(8,128)S(1)} collective-permute-done((f32[2,32,256]{2,1,0:T(8,128)S(1)}, f32[2,32,256]{2,1,0:T(8,128)S(1)}, u32[]{:S(2)}, u32[]{:S(2)}) %collective-permute-start.11) | collective-permute-done | bytes 65568 | tf_op jit(solution)/shard_map/ppermute | solution.py:466
  89.3 0.3 collective-permute-start.12
  89.6 5.3 %collective-permute-done.12 = f32[2,32,256]{2,1,0:T(8,128)S(1)} collective-permute-done((f32[2,32,256]{2,1,0:T(8,128)S(1)}, f32[2,32,256]{2,1,0:T(8,128)S(1)}, u32[]{:S(2)}, u32[]{:S(2)}) %collective-permute-start.12) | collective-permute-done | bytes 65568 | tf_op jit(solution)/shard_map/ppermute | solution.py:466
  94.9 0.3 collective-permute-start.13
  95.2 4.2 %collective-permute-done.13 = f32[2,32,256]{2,1,0:T(8,128)S(1)} collective-permute-done((f32[2,32,256]{2,1,0:T(8,128)S(1)}, f32[2,32,256]{2,1,0:T(8,128)S(1)}, u32[]{:S(2)}, u32[]{:S(2)}) %collective-permute-start.13) | collective-permute-done | bytes 65568 | tf_op jit(solution)/shard_map/ppermute | solution.py:466
  99.4 3.0 %collective-permute-start.14 = (f32[2,32,256]{2,1,0:T(8,128)S(1)}, f32[2,32,256]{2,1,0:T(8,128)S(1)}, u32[]{:S(2)}, u32[]{:S(2)}) collective-permute-start(f32[2,32,256]{2,1,0:T(8,128)S(1)} %add.52), channel_id=1, source_target_pairs={{0,160},{32,128},{64,224},{96,192},{160,0},{128,32},{224,64},{192,... | collective-permute-start | bytes 196616 | tf_op jit(solution)/shard_map/ppermute | solution.py:466
  102.4 3.6 %factor.1 = (bf16[2,2,256,1024]{3,2,1,0:T(8,128)(2,1)S(1)}, f32[2,4,128]{2,1,0:T(4,128)S(1)}) custom-call(s32[1]{0:T(128)} %bitcast.owner_ref, f32[2,32,256]{2,1,0:T(8,128)S(1)} %add.48.sums_ref), custom_call_target="tpu_custom_call" | custom-call | flops 1073741824 | bytes 4194304 | tf_op jit(solution)/shard_map/factor/pallas_call | solution.py:339
  106.1 0.7 collective-permute-done.14
  106.8 4.2 %collective-permute-start.15 = (f32[2,32,256]{2,1,0:T(8,128)S(1)}, f32[2,32,256]{2,1,0:T(8,128)S(1)}, u32[]{:S(2)}, u32[]{:S(2)}) collective-permute-start(f32[2,32,256]{2,1,0:T(8,128)S(1)} %add.53), channel_id=1, source_target_pairs={{32,64},{96,128},{160,192},{224,0},{64,32},{128,96},{192,160},{0,2... | collective-permute-start | bytes 196616 | tf_op jit(solution)/shard_map/ppermute | solution.py:466
  111.0 3.0 %apply.2.rest_3_ = bf16[32,2,32,1536]{3,2,1,0:T(8,128)(2,1)} custom-call(bf16[2,2,256,1024]{3,2,1,0:T(8,128)(2,1)S(1)} %get-tuple-element.28.maps_ref, bf16[2,2,128,1536]{3,2,1,0:T(8,128)(2,1)S(1)} %bitcast.9, bf16[2,2,32,1536]{3,2,1,0:T(8,128)(2,1)S(1)} %collective-permute-done.rest_1_, bf16[2,2,96,1536]{3,2,1,0:T(8,128)(2,1)S(1)} %collective-permute-done.2.rest_2_), custom_call_target="tpu_custom_call" | custom-call | flops 1610612736 | bytes 4194304 | tf_op jit(solution)/shard_map/apply/pallas_call | solution.py:396
  114.0 0.0 collective-permute-done.15
  114.0 3.1 %collective-permute-start.16 = (f32[2,32,256]{2,1,0:T(8,128)S(1)}, f32[2,32,256]{2,1,0:T(8,128)S(1)}, u32[]{:S(2)}, u32[]{:S(2)}) collective-permute-start(f32[2,32,256]{2,1,0:T(8,128)S(1)} %add.54), channel_id=1, source_target_pairs={{0,4},{4,0},{1,5},{5,1},{2,6},{6,2},{3,7},{7,3},{8,12},{12,8},{9,1... | collective-permute-start | bytes 196616 | tf_op jit(solution)/shard_map/ppermute | solution.py:466
  117.1 3.0 %apply.3.rest_2_ = bf16[32,2,32,1536]{3,2,1,0:T(8,128)(2,1)} custom-call(bf16[2,2,256,1024]{3,2,1,0:T(8,128)(2,1)S(1)} %get-tuple-element.28.maps_ref, bf16[2,2,128,1536]{3,2,1,0:T(8,128)(2,1)S(1)} %bitcast.10, bf16[2,2,32,1536]{3,2,1,0:T(8,128)(2,1)S(1)} %collective-permute-done.rest_1_, ...), custom_call_target="tpu_custom_call", output_to_operand_aliasing={{}: (4, {})} | custom-call | flops 1610612736 | bytes 4194304 | tf_op jit(solution)/shard_map/apply/pallas_call | solution.py:396
  120.1 0.0 collective-permute-done.16
  120.1 8.6 %solve.1 = (bf16[32,2,32,1536]{3,2,1,0:T(8,128)(2,1)}, f32[2,4,128]{2,1,0:T(4,128)S(1)}) custom-call(s32[1]{0:T(128)} %bitcast.owner_ref, f32[2,32,256]{2,1,0:T(8,128)S(1)} %add.55.sums_ref, bf16[2,2,128,1536]{3,2,1,0:T(8,128)(2,1)S(1)} %bitcast.12, bf16[2,2,128,1536]{3,2,1,0:T(8,128)(2,1)S(1)} %collective-permute-done.1.rest_1_, ...), custom_call_target="tpu_custom_call", output_to_operand_aliasing={{0}: (4, {})} | custom-call | flops 3221225472 | bytes 8388608 | tf_op jit(solution)/shard_map/solve/pallas_call | solution.py:413
  128.8 0.1 reshape.38
  128.9 0.7 copy.10
  (16 shorter events, 0.1 us)
Async XLA Ops:
  3.1 12.3 %copy-start.1 = (bf16[2,192,256]{2,1,0:T(8,128)(2,1)S(1)}, bf16[2,192,256]{2,1,0:T(8,128)(2,1)}, u32[]{:S(2)}) copy-start(bf16[2,192,256]{2,1,0:T(8,128)(2,1)} %constant.9.clone.table_ref) | copy-start | bytes 589828
  3.1 12.3 %collective-permute-start = (bf16[2,2,32,1536]{3,2,1,0:T(8,128)(2,1)}, bf16[2,2,32,1536]{3,2,1,0:T(8,128)(2,1)S(1)}, u32[]{:S(2)}, u32[]{:S(2)}) collective-permute-start(bf16[2,2,32,1536]{3,2,1,0:T(8,128)(2,1)} %bitcast.16), channel_id=1, source_target_pairs={{0,1},{1,0},{2,3},{3,2},{4,5},{5,4},{6,7},{7,6},{8,9},{9,8},{10,11... | collective-permute-start | bytes 1179656 | tf_op jit(solution)/shard_map/ppermute | solution.py:478
  9.0 31.7 %collective-permute-start.2 = (bf16[2,2,96,1536]{3,2,1,0:T(8,128)(2,1)}, bf16[2,2,96,1536]{3,2,1,0:T(8,128)(2,1)S(1)}, u32[]{:S(2)}, u32[]{:S(2)}) collective-permute-start(bf16[2,2,96,1536]{3,2,1,0:T(8,128)(2,1)} %bitcast.14), channel_id=1, source_target_pairs={{0,1},{1,0},{2,3},{3,2},{4,5},{5,4},{6,7},{7,6},{8,9},{9,8},{10,11... | collective-permute-start | bytes 3538952 | tf_op jit(solution)/shard_map/ppermute | solution.py:478
  15.4 2.8 %copy-start = (bf16[16,128,1536]{2,1,0:T(8,128)(2,1)S(1)}, bf16[16,128,1536]{2,1,0:T(8,128)(2,1)}, u32[]{:S(2)}) copy-start(bf16[16,128,1536]{2,1,0:T(8,128)(2,1)} %record_ref.3) | copy-start | bytes 18874372
  18.2 4.5 %copy-start.2 = (f32[1536]{0:T(1024)S(1)}, f32[1536]{0:T(1024)}, u32[]{:S(2)}) copy-start(f32[1536]{0:T(1024)} %param.6) | copy-start | bytes 18436
  21.1 60.4 %collective-permute-start.1 = (bf16[2,2,128,1536]{3,2,1,0:T(8,128)(2,1)S(1)}, bf16[2,2,128,1536]{3,2,1,0:T(8,128)(2,1)S(1)}, u32[]{:S(2)}, u32[]{:S(2)}) collective-permute-start(bf16[2,2,128,1536]{3,2,1,0:T(8,128)(2,1)S(1)} %bitcast.13), channel_id=1, source_target_pairs={{0,1},{1,0},{2,3},{3,2},{4,5},{5,4},{6,7},{7,6},{8,9},{9,8},{10,11... | collective-permute-start | bytes 4718600 | tf_op jit(solution)/shard_map/ppermute | solution.py:478
  42.7 1.3 %collective-permute-start.3 = (f32[2,32,256]{2,1,0:T(8,128)S(1)}, f32[2,32,256]{2,1,0:T(8,128)S(1)}, u32[]{:S(2)}, u32[]{:S(2)}) collective-permute-start(f32[2,32,256]{2,1,0:T(8,128)S(1)} %gram.2), channel_id=1, source_target_pairs={{0,2},{2,0},{1,3},{3,1},{4,6},{6,4},{5,7},{7,5},{8,10},{10,8},{9,1... | collective-permute-start | bytes 196616 | tf_op jit(solution)/shard_map/ppermute | solution.py:466
  44.1 4.4 %collective-permute-start.4 = (f32[2,32,256]{2,1,0:T(8,128)S(1)}, f32[2,32,256]{2,1,0:T(8,128)S(1)}, u32[]{:S(2)}, u32[]{:S(2)}) collective-permute-start(f32[2,32,256]{2,1,0:T(8,128)S(1)} %add.42), channel_id=1, source_target_pairs={{0,8},{16,24},{8,0},{24,16},{1,9},{17,25},{9,1},{25,17},{2,10},{18... | collective-permute-start | bytes 196616 | tf_op jit(solution)/shard_map/ppermute | solution.py:466
  48.5 5.6 %collective-permute-start.5 = (f32[2,32,256]{2,1,0:T(8,128)S(1)}, f32[2,32,256]{2,1,0:T(8,128)S(1)}, u32[]{:S(2)}, u32[]{:S(2)}) collective-permute-start(f32[2,32,256]{2,1,0:T(8,128)S(1)} %add.43), channel_id=1, source_target_pairs={{0,24},{8,16},{24,0},{16,8},{1,25},{9,17},{25,1},{17,9},{2,26},{10... | collective-permute-start | bytes 196616 | tf_op jit(solution)/shard_map/ppermute | solution.py:466
  54.0 4.4 %collective-permute-start.6 = (f32[2,32,256]{2,1,0:T(8,128)S(1)}, f32[2,32,256]{2,1,0:T(8,128)S(1)}, u32[]{:S(2)}, u32[]{:S(2)}) collective-permute-start(f32[2,32,256]{2,1,0:T(8,128)S(1)} %add.44), channel_id=1, source_target_pairs={{0,32},{64,96},{128,160},{192,224},{32,0},{96,64},{160,128},{224,1... | collective-permute-start | bytes 196616 | tf_op jit(solution)/shard_map/ppermute | solution.py:466
  58.4 9.8 %collective-permute-start.7 = (f32[2,32,256]{2,1,0:T(8,128)S(1)}, f32[2,32,256]{2,1,0:T(8,128)S(1)}, u32[]{:S(2)}, u32[]{:S(2)}) collective-permute-start(f32[2,32,256]{2,1,0:T(8,128)S(1)} %add.45), channel_id=1, source_target_pairs={{0,160},{32,128},{64,224},{96,192},{160,0},{128,32},{224,64},{192,... | collective-permute-start | bytes 196616 | tf_op jit(solution)/shard_map/ppermute | solution.py:466
  68.2 6.5 %collective-permute-start.8 = (f32[2,32,256]{2,1,0:T(8,128)S(1)}, f32[2,32,256]{2,1,0:T(8,128)S(1)}, u32[]{:S(2)}, u32[]{:S(2)}) collective-permute-start(f32[2,32,256]{2,1,0:T(8,128)S(1)} %add.46), channel_id=1, source_target_pairs={{32,64},{96,128},{160,192},{224,0},{64,32},{128,96},{192,160},{0,2... | collective-permute-start | bytes 196616 | tf_op jit(solution)/shard_map/ppermute | solution.py:466
  74.7 6.8 %collective-permute-start.9 = (f32[2,32,256]{2,1,0:T(8,128)S(1)}, f32[2,32,256]{2,1,0:T(8,128)S(1)}, u32[]{:S(2)}, u32[]{:S(2)}) collective-permute-start(f32[2,32,256]{2,1,0:T(8,128)S(1)} %add.47), channel_id=1, source_target_pairs={{0,36},{32,4},{64,100},{96,68},{128,164},{160,132},{192,228},{224,... | collective-permute-start | bytes 196616 | tf_op jit(solution)/shard_map/ppermute | solution.py:466
  83.6 1.3 %collective-permute-start.10 = (f32[2,32,256]{2,1,0:T(8,128)S(1)}, f32[2,32,256]{2,1,0:T(8,128)S(1)}, u32[]{:S(2)}, u32[]{:S(2)}) collective-permute-start(f32[2,32,256]{2,1,0:T(8,128)S(1)} %gram.3), channel_id=1, source_target_pairs={{0,2},{2,0},{1,3},{3,1},{4,6},{6,4},{5,7},{7,5},{8,10},{10,8},{9,1... | collective-permute-start | bytes 196616 | tf_op jit(solution)/shard_map/ppermute | solution.py:466
  84.9 4.4 %collective-permute-start.11 = (f32[2,32,256]{2,1,0:T(8,128)S(1)}, f32[2,32,256]{2,1,0:T(8,128)S(1)}, u32[]{:S(2)}, u32[]{:S(2)}) collective-permute-start(f32[2,32,256]{2,1,0:T(8,128)S(1)} %add.49), channel_id=1, source_target_pairs={{0,8},{16,24},{8,0},{24,16},{1,9},{17,25},{9,1},{25,17},{2,10},{18... | collective-permute-start | bytes 196616 | tf_op jit(solution)/shard_map/ppermute | solution.py:466
  89.3 5.6 %collective-permute-start.12 = (f32[2,32,256]{2,1,0:T(8,128)S(1)}, f32[2,32,256]{2,1,0:T(8,128)S(1)}, u32[]{:S(2)}, u32[]{:S(2)}) collective-permute-start(f32[2,32,256]{2,1,0:T(8,128)S(1)} %add.50), channel_id=1, source_target_pairs={{0,24},{8,16},{24,0},{16,8},{1,25},{9,17},{25,1},{17,9},{2,26},{10... | collective-permute-start | bytes 196616 | tf_op jit(solution)/shard_map/ppermute | solution.py:466
  94.9 4.5 %collective-permute-start.13 = (f32[2,32,256]{2,1,0:T(8,128)S(1)}, f32[2,32,256]{2,1,0:T(8,128)S(1)}, u32[]{:S(2)}, u32[]{:S(2)}) collective-permute-start(f32[2,32,256]{2,1,0:T(8,128)S(1)} %add.51), channel_id=1, source_target_pairs={{0,32},{64,96},{128,160},{192,224},{32,0},{96,64},{160,128},{224,1... | collective-permute-start | bytes 196616 | tf_op jit(solution)/shard_map/ppermute | solution.py:466
  99.4 7.4 %collective-permute-start.14 = (f32[2,32,256]{2,1,0:T(8,128)S(1)}, f32[2,32,256]{2,1,0:T(8,128)S(1)}, u32[]{:S(2)}, u32[]{:S(2)}) collective-permute-start(f32[2,32,256]{2,1,0:T(8,128)S(1)} %add.52), channel_id=1, source_target_pairs={{0,160},{32,128},{64,224},{96,192},{160,0},{128,32},{224,64},{192,... | collective-permute-start | bytes 196616 | tf_op jit(solution)/shard_map/ppermute | solution.py:466
  106.8 7.2 %collective-permute-start.15 = (f32[2,32,256]{2,1,0:T(8,128)S(1)}, f32[2,32,256]{2,1,0:T(8,128)S(1)}, u32[]{:S(2)}, u32[]{:S(2)}) collective-permute-start(f32[2,32,256]{2,1,0:T(8,128)S(1)} %add.53), channel_id=1, source_target_pairs={{32,64},{96,128},{160,192},{224,0},{64,32},{128,96},{192,160},{0,2... | collective-permute-start | bytes 196616 | tf_op jit(solution)/shard_map/ppermute | solution.py:466
  114.0 6.1 %collective-permute-start.16 = (f32[2,32,256]{2,1,0:T(8,128)S(1)}, f32[2,32,256]{2,1,0:T(8,128)S(1)}, u32[]{:S(2)}, u32[]{:S(2)}) collective-permute-start(f32[2,32,256]{2,1,0:T(8,128)S(1)} %add.54), channel_id=1, source_target_pairs={{0,4},{4,0},{1,5},{5,1},{2,6},{6,2},{3,7},{7,3},{8,12},{12,8},{9,1... | collective-permute-start | bytes 196616 | tf_op jit(solution)/shard_map/ppermute | solution.py:466

commit v2 on v1

v2 whole, which is shorter than its diff:
```python
import functools
import math

import jax
import jax.numpy as jnp
import numpy as np
from jax import lax
from jax.experimental import pallas as pl
from jax.experimental.pallas import tpu as pltpu
from jax.sharding import Mesh
from jax.sharding import PartitionSpec as P

NF = 64
NT = 128
GROUPS = (1, 1, 2)
FINE = ("z", "y", "xh", "core", "blk")
AHEAD = 3
MIB = 1024 * 1024
HEAVY = 40_000_000_000


def spectral_table():
    time_index = np.arange(NT, dtype=np.int32)
    freq_index = np.arange(NF, dtype=np.int32)
    step = np.float32(2.0 * math.pi / NT)
    phases = (freq_index[:, None] * time_index[None, :] % NT).astype(np.float32) * step
    window = np.float32(0.5) - np.float32(0.5) * np.cos(time_index.astype(np.float32) * step)
    norm = np.sqrt(np.sum(window * window))
    rows_cos = window * np.cos(phases) / norm
    rows_sin = -window * np.sin(phases) / norm
    return np.stack([rows_cos, rows_sin], axis=1).astype(jnp.bfloat16)


def pair_table(first_owner):
    table = spectral_table().reshape(2, 4, 8, 2, NT)
    out = np.zeros((2, 4, 2, 2, 8, 2, NT), dtype=table.dtype)
    for b in range(2):
        out[:, :, :, b, :, b, :] = table.transpose(0, 1, 3, 2, 4)
    if first_owner:
        out = out[::-1]
    return np.ascontiguousarray(out).reshape(256, 256)


def early_kernel(first, owner_ref, tables_ref, record_ref, out_ref, table, rows, table_sem, sems):
    pairs, _, _, points = rows.shape
    head = pltpu.make_async_copy(tables_ref.at[owner_ref[0]], table, table_sem)
    head.start()
    copies = [
        pltpu.make_async_copy(
            record_ref.at[pl.ds(2 * (first + p), 2)], rows.at[p], sems.at[p]
        )
        for p in range(pairs)
    ]
    for p in range(min(4, pairs)):
        copies[p].start()
    head.wait()
    left = table[...]
    for p in range(pairs):
        copies[p].wait()
        if p + 4 < pairs:
            copies[p + 4].start()
        value = jnp.dot(
            left, rows[p].reshape(256, points), preferred_element_type=jnp.float32
        ).astype(jnp.bfloat16)
        for row in range(0, value.shape[0], 16):
            out_ref[row // 32, row // 16 % 2, p] = value[row : row + 16]


def early_call(owner, tables, record, first, pairs):
    blocks, times, points = record.shape
    count = tables.shape[1] // 32
    out = pl.pallas_call(
        functools.partial(early_kernel, first),
        in_specs=[
            pl.BlockSpec(memory_space=pltpu.SMEM),
            pl.BlockSpec(memory_space=pl.ANY),
            pl.BlockSpec(memory_space=pl.ANY),
        ],
        out_specs=pl.BlockSpec(memory_space=pltpu.VMEM),
        out_shape=jax.ShapeDtypeStruct((count, 2, pairs, 16, points), jnp.bfloat16),
        scratch_shapes=[
            pltpu.VMEM((32 * count, 256), jnp.bfloat16),
            pltpu.VMEM((pairs, 2, times, points), jnp.bfloat16),
            pltpu.SemaphoreType.DMA,
            pltpu.SemaphoreType.DMA((pairs,)),
        ],
        compiler_params=pltpu.CompilerParams(vmem_limit_bytes=58 * MIB),
        cost_estimate=pl.CostEstimate(
            flops=HEAVY // 2, bytes_accessed=pairs * MIB, transcendentals=0
        ),
        name="early",
    )(owner, tables, record)
    return out.reshape(count, 2, 16 * pairs, points)


def spectra_kernel(owner_ref, table_ref, record_ref, *outs):
    points = record_ref.shape[-1]
    width = 256
    for start in range(0, points, width):
        cols = pl.ds(start, width)
        rows = record_ref[:, :, cols].reshape(256, width)
        value = jnp.dot(table_ref[0], rows, preferred_element_type=jnp.float32)
        value = value.astype(jnp.bfloat16)
        row = 0
        for out in outs:
            for chunk in range(out.shape[0]):
                for c in range(2):
                    out[chunk, c, 0, :, cols] = value[row : row + 16]
                    row += 16


def spectra_call(owner, tables, record, chunks):
    blocks, times, points = record.shape
    pairs = blocks // 2
    count = tables.shape[1] // 32
    outs = pl.pallas_call(
        spectra_kernel,
        grid_spec=pltpu.PrefetchScalarGridSpec(
            num_scalar_prefetch=1,
            grid=(pairs,),
            in_specs=[
                pl.BlockSpec((1, 32 * count, 256), lambda p, owner: (owner[0], 0, 0)),
                pl.BlockSpec((2, times, points), lambda p, owner: (p, 0, 0)),
            ],
            out_specs=[
                pl.BlockSpec((n, 2, 1, 16, points), lambda p, owner: (0, 0, p, 0, 0))
                for n in chunks
            ],
        ),
        out_shape=[
            jax.ShapeDtypeStruct((n, 2, pairs, 16, points), jnp.bfloat16) for n in chunks
        ],
        compiler_params=pltpu.CompilerParams(vmem_limit_bytes=16 * MIB),
        cost_estimate=pl.CostEstimate(
            flops=HEAVY, bytes_accessed=(6 + count) * MIB, transcendentals=0
        ),
        name="spectra",
    )(owner, tables, record)
    return [out.reshape(n, 2, 16 * pairs, points) for n, out in zip(chunks, outs)]


def nt_dot(a, b):
    return lax.dot_general(a, b, (((1,), (1,)), ((), ())), preferred_element_type=jnp.float32)


def swap_rows(x):
    half = x.shape[0] // 2
    return jnp.concatenate([x[half:], x[:half]], axis=0)


def swap_lanes(x):
    half = x.shape[1] // 2
    return jnp.concatenate([x[:, half:], x[:, :half]], axis=1)


def upper():
    row = lax.broadcasted_iota(jnp.int32, (32, 256), 0)
    return row >= lax.broadcasted_iota(jnp.int32, (32, 256), 1) // 8


def unpack(packed):
    row_f = lax.broadcasted_iota(jnp.int32, (32, 8, 256), 1)
    same = row_f == lax.broadcasted_iota(jnp.int32, (32, 8, 256), 2) % 8
    spread = jnp.where(same, jnp.broadcast_to(packed[:, None, :], (32, 8, 256)), 0.0)
    turned = spread.reshape(256, 256).T.reshape(32, 8, 256).sum(axis=1)
    row = lax.broadcasted_iota(jnp.int32, (32, 256), 0)
    column = lax.broadcasted_iota(jnp.int32, (32, 256), 1) // 8
    real = jnp.where(row >= column, packed, turned)
    imag = jnp.where(row < column, packed, jnp.where(row > column, -turned, 0.0))
    return real, imag


def chunk_rows(refs, parts, c):
    return jnp.concatenate([refs[ref][chunk, c] for ref, chunk in parts], axis=0)


def gram_kernel(plan, prior, owner_ref, core_ref, weights_ref, *refs):
    first = owner_ref[0] == 0
    weights = weights_ref[...]
    row_f = lax.broadcasted_iota(jnp.int32, (256, 256), 0) % 8
    col_f = lax.broadcasted_iota(jnp.int32, (256, 256), 1) % 8
    same = row_f == col_f
    packed = [refs[-3][0]] if prior else []
    for parts in plan:
        x0, x1 = (chunk_rows(refs, parts, c) for c in range(2))
        w0 = (x0.astype(jnp.float32) * weights).astype(jnp.bfloat16)
        w1 = (x1.astype(jnp.float32) * weights).astype(jnp.bfloat16)
        real = nt_dot(x0, w0) + nt_dot(x1, w1)
        imag = nt_dot(x0, w1) - nt_dot(x1, w0)
        both = []
        for value in (real, imag):
            value = jnp.where(same, value, 0.0).reshape(32, 8, 256).sum(axis=1)
            both.append(jnp.where(first, value, swap_rows(swap_lanes(value))))
        packed.append(jnp.where(upper(), both[0], both[1]))
    if len(packed) == 1:
        refs[-1][0] = packed[0]
    else:
        core = core_ref[0] == 0
        refs[-2][0] = jnp.where(core, packed[0], packed[1])
        refs[-1][0] = jnp.where(core, packed[1], packed[0])


def plan_of(rows):
    arrays = []
    for parts in rows:
        for array, _ in parts:
            if not any(array is other for other in arrays):
                arrays.append(array)
    index = lambda array: next(i for i, other in enumerate(arrays) if other is array)
    return arrays, [[(index(array), chunk) for array, chunk in parts] for parts in rows]


def gram_call(place, weights, rows, prior=None, flops=1 << 30):
    arrays, plan = plan_of(rows)
    points = arrays[0].shape[-1]
    results = len(rows) + (prior is not None)
    operands = [*place, weights, *arrays]
    if prior is not None:
        operands.append(prior)
    return pl.pallas_call(
        functools.partial(gram_kernel, plan, prior is not None),
        in_specs=[pl.BlockSpec(memory_space=pltpu.SMEM)] * 2
        + [pl.BlockSpec(memory_space=pltpu.VMEM)] * (len(operands) - 2),
        out_specs=[pl.BlockSpec(memory_space=pltpu.VMEM)] * results,
        out_shape=[jax.ShapeDtypeStruct((1, 32, 256), jnp.float32)] * results,
        compiler_params=pltpu.CompilerParams(vmem_limit_bytes=16 * MIB),
        cost_estimate=pl.CostEstimate(
            flops=flops,
            bytes_accessed=2 * MIB * len(rows),
            transcendentals=0,
        ),
        name="gram",
    )(*operands)


def eliminate(products, scale):
    lane = lax.broadcasted_iota(jnp.int32, (8, 128), 1)
    lane_f = lane % 8
    lane_row = lane // 8
    sub = lax.broadcasted_iota(jnp.int32, (8, 128), 0)
    states = []
    for real, imag in products:
        real, imag = real * scale, imag * scale
        grid = []
        for q in range(4):
            half = slice(128 * (q % 2), 128 * (q % 2) + 128)
            top, bottom = (real, imag) if q < 2 else (-imag, real)
            grid.append(
                [top[8 * s : 8 * s + 8, half] for s in range(4)]
                + [bottom[8 * s : 8 * s + 8, half] for s in range(4)]
            )
        states.append(grid)
    def column_of(grid, k):
        take = lane_f + 8 * (k % 16)
        return [
            jnp.take_along_axis(grid[k // 16][s], take, axis=1, mode="promise_in_bounds")
            for s in range(8)
        ]

    def row_of(blocks, k):
        return jnp.broadcast_to(blocks[k // 8][k % 8 : k % 8 + 1], (8, 128))

    ahead = [{k: column_of(grid, k) for k in range(AHEAD)} for grid in states]
    for k in range(64):
        q0, group = divmod(k, 16)
        s0, r0 = divmod(k, 8)
        for grid, later in zip(states, ahead):
            column = later.pop(k)
            if k + AHEAD < 64:
                later[k + AHEAD] = column_of(grid, k + AHEAD)
            inverse = 1.0 / row_of(column, k)
            factors = {n: row_of(column, n) * inverse for n in later}
            column[s0] = jnp.where(sub == r0, 1.0, column[s0])
            for n, blocks in later.items():
                blocks[s0] = jnp.where(sub == r0, 0.0, blocks[s0])
                later[n] = [blocks[s] - column[s] * factors[n] for s in range(8)]
            for q in range(q0, 4):
                factor = row_of(grid[q], k) * inverse
                keep = sub != r0
                if q == q0:
                    factor = jnp.where(lane_row > group, factor, 0.0)
                    keep = keep | (lane_row <= group)
                grid[q][s0] = jnp.where(keep, grid[q][s0], 0.0)
                for s in range(8):
                    grid[q][s] = grid[q][s] - column[s] * factor
    return states


def diagonal(grid):
    lane_row = lax.broadcasted_iota(jnp.int32, (8, 128), 1) // 8
    sub = lax.broadcasted_iota(jnp.int32, (8, 128), 0)
    out = []
    for q in range(4):
        total = jnp.zeros((8, 128), jnp.float32)
        for s in (2 * q, 2 * q + 1):
            total = total + jnp.where(lane_row + 16 * q == sub + 8 * s, grid[q][s], 0.0)
        out.append(total.sum(axis=0, keepdims=True))
    return out


def lower_rows(grid, pivots):
    lane_row = lax.broadcasted_iota(jnp.int32, (8, 128), 1) // 8
    sub = lax.broadcasted_iota(jnp.int32, (8, 128), 0)
    halves = []
    for q in (2, 3):
        root = lax.rsqrt(pivots[q])
        blocks = []
        for s in range(8):
            row, column = lane_row + 16 * q, sub + 8 * s
            value = jnp.where(column < row, grid[q][s], jnp.where(column == row, 1.0, 0.0))
            blocks.append(value * root)
        halves.append(jnp.concatenate(blocks, axis=0))
    return jnp.concatenate(halves, axis=1)


def by_frequency(pivots):
    sub = lax.broadcasted_iota(jnp.int32, (8, 128), 0)
    lane = lax.broadcasted_iota(jnp.int32, (8, 128), 1)
    out = jnp.zeros((8, 128), jnp.float32)
    for q, vector in enumerate(pivots):
        wide = jnp.broadcast_to(vector, (8, 128))
        turned = jnp.take_along_axis(
            wide, lane % 16 * 8 + sub, axis=1, mode="promise_in_bounds"
        )
        out = jnp.where(lane // 16 == q, turned, out)
    return out[:, :64]


def factor_kernel(scale, sums_ref, out_ref):
    grid = eliminate([unpack(sums_ref[0])], scale)[0]
    pivots = diagonal(grid)
    out_ref[:64, :] = lower_rows(grid, pivots)
    out_ref[64:, :] = jnp.zeros((8, 256), jnp.float32)
    out_ref[64:, :64] = by_frequency(pivots)


def factor_call(sums, point_count):
    return pl.pallas_call(
        functools.partial(factor_kernel, 1.0 / point_count),
        in_specs=[pl.BlockSpec(memory_space=pltpu.VMEM)],
        out_specs=pl.BlockSpec(memory_space=pltpu.VMEM),
        out_shape=jax.ShapeDtypeStruct((72, 256), jnp.float32),
        compiler_params=pltpu.CompilerParams(vmem_limit_bytes=16 * MIB),
        cost_estimate=pl.CostEstimate(flops=1 << 30, bytes_accessed=4 * MIB, transcendentals=0),
        name="factor",
    )(sums)


def build_maps(owner, full, maps_ref):
    out_row = lax.broadcasted_iota(jnp.int32, (256, 256), 0)
    lane = lax.broadcasted_iota(jnp.int32, (256, 256), 1)
    same = out_row // 32 == lane % 8
    order = (same & (out_row % 32 == lane // 8)).astype(jnp.bfloat16)
    b_row = lax.broadcasted_iota(jnp.int32, (32, 256), 0)
    b_lane = lax.broadcasted_iota(jnp.int32, (32, 256), 1) // 8
    spread = (b_row == (b_lane + 16 * owner) % 32).astype(jnp.bfloat16)
    high = full.astype(jnp.bfloat16)
    low = (full - high.astype(jnp.float32)).astype(jnp.bfloat16)
    for level, value in enumerate((high, low)):
        rows = nt_dot(order, value).astype(jnp.bfloat16)
        for c in range(2):
            wide = jnp.dot(
                rows[:, 32 * c : 32 * c + 32], spread, preferred_element_type=jnp.float32
            )
            wide = jnp.where(same, wide, 0.0)
            at = 256 * (2 * c + level)
            maps_ref[0, :, at : at + 256] = (wide if c == 0 else -wide).astype(jnp.bfloat16)
            at = 256 * (2 * (1 - c) + level)
            maps_ref[1, :, at : at + 256] = wide.astype(jnp.bfloat16)


def apply_kernel(base, theirs, plan, energies, owner_ref, core_ref, full_ref, *refs):
    count = max(ref for parts in plan for ref, _ in parts) + 1
    rows, refs = refs[:count], refs[count:]
    if energies:
        others, (modes_ref, energies_ref, small_ref, small_sem) = refs[:3], refs[-7:-3]
    else:
        modes_ref = refs[-4]
    maps_ref, held_ref, sems = refs[-3:]
    core = core_ref[0]
    chosen = 1 - core if theirs else core
    copies = []
    if energies:
        for half, pair in enumerate(((others[0], others[1]), (others[2], full_ref))):
            values = [ref[64:, :64] for ref in pair]
            at = 16 * half
            small_ref[at : at + 8, :] = jnp.where(core == 0, values[0], values[1])
            small_ref[at + 8 : at + 16, :] = jnp.where(core == 0, values[1], values[0])
        copies.append(pltpu.make_async_copy(small_ref, energies_ref, small_sem))
        copies[0].start()
    build_maps(owner_ref[0], full_ref[:64, :], maps_ref)
    points = held_ref.shape[-1]
    width = 256
    piece = points // sems.shape[0]
    target = modes_ref.at[pl.ds(8 * (base + chosen), 8)]
    for part in range(sems.shape[0]):
        for start in range(part * piece, (part + 1) * piece, width):
            cols = pl.ds(start, width)
            x0, x1 = (
                jnp.concatenate(
                    [
                        rows[ref][chosen, c, :, cols]
                        if rows[ref].shape[0] == 2
                        else jnp.where(
                            chosen == 0, rows[ref][0, c, :, cols], rows[other][0, c, :, cols]
                        )
                        for (ref, _), (other, _) in zip(*plan)
                    ],
                    axis=0,
                )
                for c in range(2)
            )
            stacked = jnp.concatenate([x0, x0, x1, x1], axis=0)
            for c in range(2):
                value = jnp.dot(maps_ref[c], stacked, preferred_element_type=jnp.float32)
                held_ref[:, c, :, cols] = value.astype(jnp.bfloat16).reshape(8, 32, width)
        cols = pl.ds(part * piece, piece)
        copy = pltpu.make_async_copy(
            held_ref.at[:, :, :, cols], target.at[:, :, :, cols], sems.at[part]
        )
        copy.start()
        copies.append(copy)
    for copy in copies:
        copy.wait()


def modes_shape(total_chunks, points):
    return jax.ShapeDtypeStruct((8 * total_chunks, 2, 32, points), jnp.bfloat16)


def apply_call(place, full, rows, modes, base, theirs, total_chunks, others=()):
    arrays, plan = plan_of(rows)
    points = arrays[0].shape[-1]
    operands = [*place, full, *arrays, *others]
    in_specs = [pl.BlockSpec(memory_space=pltpu.SMEM)] * 2
    in_specs += [pl.BlockSpec(memory_space=pltpu.VMEM)] * (len(operands) - 2)
    aliases, small = {}, []
    if modes is not None:
        aliases = {len(operands): 0}
        in_specs.append(pl.BlockSpec(memory_space=pl.ANY))
        operands.append(modes)
    out_specs = [pl.BlockSpec(memory_space=pl.ANY)]
    out_shape = [modes_shape(total_chunks, points)]
    if others:
        out_specs.append(pl.BlockSpec(memory_space=pl.ANY))
        out_shape.append(jax.ShapeDtypeStruct((8 * total_chunks, 64), jnp.float32))
        small = [pltpu.VMEM((8 * total_chunks, 64), jnp.float32), pltpu.SemaphoreType.DMA]
    return pl.pallas_call(
        functools.partial(apply_kernel, base, theirs, plan, bool(others)),
        in_specs=in_specs,
        out_specs=out_specs,
        out_shape=out_shape,
        scratch_shapes=small
        + [
            pltpu.VMEM((2, 256, 1024), jnp.bfloat16),
            pltpu.VMEM((8, 2, 32, points), jnp.bfloat16),
            pltpu.SemaphoreType.DMA((6,)),
        ],
        input_output_aliases=aliases,
        compiler_params=pltpu.CompilerParams(vmem_limit_bytes=16 * MIB),
        cost_estimate=pl.CostEstimate(
            flops=16 * 256 * 256 * points, bytes_accessed=4 * MIB, transcendentals=0
        ),
        name="apply",
    )(*operands)


def after(value, *others):
    return lax.optimization_barrier((value, *others))[0]


def involution(pairs):
    return pairs + [(b, a) for a, b in pairs]


CORE = ("core", involution([(0, 1)]))
STEPS = (
    ("y", involution([(0, 1), (2, 3)])),
    ("y", involution([(0, 3), (1, 2)])),
    ("z", involution([(0, 1), (2, 3), (4, 5), (6, 7)])),
    ("z", involution([(0, 2), (1, 3), (4, 6), (5, 7)])),
    ("z", involution([(0, 7), (1, 6), (2, 5), (3, 4)])),
    ("xh", involution([(0, 1)])),
)


def add_step(value, step):
    axis, pairs = step
    return value + lax.ppermute(value, axis, pairs)


def local(record, weights):
    points = record.shape[-1]
    space = 1
    for axis in FINE[:-1]:
        space *= lax.axis_size(axis)
    owner, core = (
        lax.axis_index(axis).astype(jnp.int32).reshape(1) for axis in ("blk", "core")
    )
    place = (owner, core)
    wide = weights.reshape(1, points)
    tables = np.stack([pair_table(0), pair_table(1)])
    part = lambda a, b: jnp.asarray(tables[:, a:b])
    swap = lambda s: lax.ppermute(s, "blk", [(0, 1), (1, 0)])
    cross = lambda value: lax.ppermute(value, *CORE)
    gram = functools.partial(gram_call, place, wide)

    away_a = early_call(owner, part(128, 192), record, 0, 2)
    peer_a = swap(away_a)
    away_b = early_call(owner, part(128, 192), after(record, away_a), 2, 6)
    peer_b = swap(away_b)
    rest = np.concatenate([tables[:, 192:], tables[:, :128]], axis=1)
    away_c, away_d, own_ab, own_cd = spectra_call(
        owner, jnp.asarray(rest), after(record, peer_a, away_b), (1, 1, 2, 2)
    )
    peer_c, peer_d = swap(away_c), swap(away_d)
    rows_ab = [[(own_ab, i), (peer_a, i), (peer_b, i)] for i in range(2)]

    apply = functools.partial(apply_call, place, total_chunks=4)

    ab, other = gram(rows_ab, flops=HEAVY)
    ab = ab + cross(other)
    for step in STEPS[:4]:
        ab = add_step(ab, step)
    peer_c = after(peer_c, ab)
    c = gram([[(own_cd, 0), (peer_c, 0)]])[0]
    ab = add_step(ab, STEPS[4])
    peer_d = after(peer_d, ab)
    cd, other = gram([[(own_cd, 1), (peer_d, 0)]], c)
    rows_cd = [[(own_cd, 0), (peer_c, 0)], [(own_cd, 1), (peer_d, 0)]]
    ab = add_step(ab, STEPS[5])
    cd = cd + cross(other)
    cd = add_step(cd, STEPS[0])
    mine_ab = factor_call(after(ab, cd), points * space)
    theirs_ab = cross(mine_ab)
    for step in STEPS[1:3]:
        cd = add_step(cd, step)
    modes = apply(after(mine_ab, cd), rows_ab, None, 0, False)[0]
    cd = add_step(after(cd, mine_ab), STEPS[3])
    modes = apply(after(theirs_ab, cd), rows_ab, modes, 0, True)[0]
    for step in STEPS[4:]:
        cd = add_step(cd, step)
    mine_cd = factor_call(cd, points * space)
    theirs_cd = cross(mine_cd)
    modes = apply(mine_cd, rows_cd, modes, 2, False)[0]
    return tuple(
        apply(theirs_cd, rows_cd, modes, 2, True, others=(mine_ab, theirs_ab, mine_cd))
    )


def solution(mesh):
    fine = Mesh(mesh.devices.reshape(8, 4, 2, 2, 2), FINE)
    return jax.shard_map(
        local,
        mesh=fine,
        in_specs=(P("blk", None, FINE[:-1]), P(FINE[:-1])),
        out_specs=(P("blk", None, None, FINE[:-1]), P("blk", None)),
        check_vma=False,
    )
```

time: 130 us -> 119 us (0.915)
  the two profiles are of different devices: /device:TPU:24 before, /device:TPU:1 now
where the time goes in v2:
time: 119 us
  starting transfers between devices  45.5 us (38%)
  waiting for transfers between devices  39.8 us (33%)
  Pallas kernels  29.3 us (25%)
  local copies, waits for them, and re-layouts  2.8 us (2%)
    ppermute x4, waiting for transfers between devices, local(): swap = lambda s: lax.ppermute(s, 'blk', [(0, 1), (1, 0)])  26.6 us
    ppermute x12, starting transfers between devices, add_step(): return value + lax.ppermute(value, axis, pairs)  25.9 us
    ppermute x4, starting transfers between devices, local(): cross = lambda value: lax.ppermute(value, *CORE)  15 us
    pallas_call x4, Pallas kernels, apply_call(): pl.pallas_call(functools.partial(apply_kernel, base, theirs, plan, bool(o...  12.1 us
    ppermute x12, waiting for transfers between devices, add_step(): return value + lax.ppermute(value, axis, pairs)  11.5 us
    pallas_call x2, Pallas kernels, early_call(): pl.pallas_call(functools.partial(early_kernel, first), in_specs=[pl.Block...  6.71 us
    ppermute x4, starting transfers between devices, local(): swap = lambda s: lax.ppermute(s, 'blk', [(0, 1), (1, 0)])  4.51 us
    pallas_call x3, Pallas kernels, gram_call(): pl.pallas_call(functools.partial(gram_kernel, plan, prior is not None), i...  4.28 us
  transfers between devices with their start and end apart: 20, of which 11 were waited for; matrix products, arithmetic and copies ran while one was open for 0% of the time, Pallas kernels for 18%

profile of v2, /device:TPU:1, one launch (start us, length us, event | category | flops | bytes accessed | tf_op | source)
XLA Modules:
  0.0 118.6 jit_solution(2887124478371843542)
XLA Ops:
  0.6 2.4 %early.2 = bf16[2,2,2,16,1536]{4,3,2,1,0:T(8,128)(2,1)} custom-call(s32[1]{0:T(128)} %bitcast.owner_ref, bf16[2,64,256]{2,1,0:T(8,128)(2,1)} %constant.10.clone.tables_ref, bf16[16,128,1536]{2,1,0:T(8,128)(2,1)} %record_ref.3), custom_call_target="tpu_custom_call" | custom-call | flops 20000000000 | bytes 2097152 | tf_op jit(solution)/shard_map/early/pallas_call | solution.py:72
  3.1 0.0 copy-start.2
  3.1 0.0 copy-start.1
  3.1 2.1 %collective-permute-start = (bf16[2,2,32,1536]{3,2,1,0:T(8,128)(2,1)}, bf16[2,2,32,1536]{3,2,1,0:T(8,128)(2,1)S(1)}, u32[]{:S(2)}, u32[]{:S(2)}) collective-permute-start(bf16[2,2,32,1536]{3,2,1,0:T(8,128)(2,1)} %bitcast.18), channel_id=1, source_target_pairs={{0,1},{1,0},{2,3},{3,2},{4,5},{5,4},{6,7},{7,6},{8,9},{9,8},{10,11... | collective-permute-start | bytes 1179656 | tf_op jit(solution)/shard_map/ppermute | solution.py:504
  5.2 4.3 %early.3 = bf16[2,2,6,16,1536]{4,3,2,1,0:T(8,128)(2,1)} custom-call(s32[1]{0:T(128)} %bitcast.owner_ref, bf16[2,64,256]{2,1,0:T(8,128)(2,1)} %constant.10.clone.tables_ref, bf16[16,128,1536]{2,1,0:T(8,128)(2,1)} %record_ref.3), custom_call_target="tpu_custom_call" | custom-call | flops 20000000000 | bytes 6291456 | tf_op jit(solution)/shard_map/early/pallas_call | solution.py:72
  9.5 0.1 collective-permute-start.2
  9.6 0.0 copy-done.2
  9.6 3.4 %collective-permute-done.refs_1_ = bf16[2,2,32,1536]{3,2,1,0:T(8,128)(2,1)S(1)} collective-permute-done((bf16[2,2,32,1536]{3,2,1,0:T(8,128)(2,1)}, bf16[2,2,32,1536]{3,2,1,0:T(8,128)(2,1)S(1)}, u32[]{:S(2)}, u32[]{:S(2)}) %collective-permute-start) | collective-permute-done | bytes 393248 | tf_op jit(solution)/shard_map/ppermute | solution.py:504
  13.0 0.0 copy-done.1
  13.0 0.0 copy-start
  13.0 2.8 %copy-done = bf16[16,128,1536]{2,1,0:T(8,128)(2,1)S(1)} copy-done((bf16[16,128,1536]{2,1,0:T(8,128)(2,1)S(1)}, bf16[16,128,1536]{2,1,0:T(8,128)(2,1)}, u32[]{:S(2)}) %copy-start) | copy-done | bytes 6291480
  15.8 3.0 %spectra.1 = (bf16[1,2,8,16,1536]{4,3,2,1,0:T(8,128)(2,1)S(1)}, bf16[1,2,8,16,1536]{4,3,2,1,0:T(8,128)(2,1)S(1)}, bf16[2,2,8,16,1536]{4,3,2,1,0:T(8,128)(2,1)S(1)}, bf16[2,2,8,16,1536]{4,3,2,1,0:T(8,128)(2,1)S(1)}) custom-call(s32[1]{0:T(128)} %bitcast.owner_ref, bf16[2,192,256]{2,1,0:T(8,128)(2,1)S(1)} %copy-done.1, bf16[16,128,1536]{2,1,0:T(8,128)(2,1)S(1)} %copy-done), custom_call_target="tpu_custom_call" | custom-call | flops 40000000000 | bytes 12582912 | tf_op jit(solution)/shard_map/spectra/pallas_call | solution.py:116
  18.8 2.2 %collective-permute-start.9 = (bf16[1,2,128,1536]{3,2,1,0:T(8,128)(2,1)S(1)}, bf16[1,2,128,1536]{3,2,1,0:T(8,128)(2,1)S(1)}, u32[]{:S(2)}, u32[]{:S(2)}) collective-permute-start(bf16[1,2,128,1536]{3,2,1,0:T(8,128)(2,1)S(1)} %bitcast.16), channel_id=1, source_target_pairs={{0,1},{1,0},{2,3},{3,2},{4,5},{5,4},{6,7},{7,6},{8,9},{9,8},{10,11... | collective-permute-start | bytes 2359304 | tf_op jit(solution)/shard_map/ppermute | solution.py:504
  21.0 0.1 collective-permute-start.1
  21.1 17.2 %collective-permute-done.2.refs_2_ = bf16[2,2,96,1536]{3,2,1,0:T(8,128)(2,1)S(1)} collective-permute-done((bf16[2,2,96,1536]{3,2,1,0:T(8,128)(2,1)}, bf16[2,2,96,1536]{3,2,1,0:T(8,128)(2,1)S(1)}, u32[]{:S(2)}, u32[]{:S(2)}) %collective-permute-start.2) | collective-permute-done | bytes 1179680 | tf_op jit(solution)/shard_map/ppermute | solution.py:504
  38.3 2.1 %gram.3 = (f32[1,32,256]{2,1,0:T(8,128)S(1)}, f32[1,32,256]{2,1,0:T(8,128)S(1)}) custom-call(s32[1]{0:T(128)} %bitcast.owner_ref, s32[1]{0:T(128)} %bitcast.1.core_ref, f32[1,1536]{1,0:T(1,128)S(1)} %reshape.33.weights_ref, bf16[2,2,128,1536]{3,2,1,0:T(8,128)(2,1)S(1)} %bitcast.12, bf16[2,2,32,1536]{3,2,1,0:T(8,128)(2,1)S(1)} %collective-permute-done.refs_1_, ...), custom_call_target="tpu_custom_call" | custom-call | flops 40000000000 | bytes 4194304 | tf_op jit(solution)/shard_map/gram/pallas_call | solution.py:220
  40.4 5.1 %collective-permute-start.3 = (f32[1,32,256]{2,1,0:T(8,128)S(1)}, f32[1,32,256]{2,1,0:T(8,128)S(1)}, u32[]{:S(2)}, u32[]{:S(2)}) collective-permute-start(f32[1,32,256]{2,1,0:T(8,128)S(1)} %get-tuple-element.24), channel_id=1, source_target_pairs={{0,2},{2,0},{1,3},{3,1},{4,6},{6,4},{5,7},{7,5},{8,10},{10,8},{9,1... | collective-permute-start | bytes 98312 | tf_op jit(solution)/shard_map/ppermute | solution.py:505
  45.4 0.9 collective-permute-done.3
  46.3 0.2 collective-permute-start.4
  46.5 2.9 %collective-permute-done.4 = f32[1,32,256]{2,1,0:T(8,128)S(1)} collective-permute-done((f32[1,32,256]{2,1,0:T(8,128)S(1)}, f32[1,32,256]{2,1,0:T(8,128)S(1)}, u32[]{:S(2)}, u32[]{:S(2)}) %collective-permute-start.4) | collective-permute-done | bytes 32800 | tf_op jit(solution)/shard_map/ppermute | solution.py:489
  49.4 1.6 %collective-permute-start.5 = (f32[1,32,256]{2,1,0:T(8,128)S(1)}, f32[1,32,256]{2,1,0:T(8,128)S(1)}, u32[]{:S(2)}, u32[]{:S(2)}) collective-permute-start(f32[1,32,256]{2,1,0:T(8,128)S(1)} %add.43), channel_id=1, source_target_pairs={{0,24},{8,16},{24,0},{16,8},{1,25},{9,17},{25,1},{17,9},{2,26},{10... | collective-permute-start | bytes 98312 | tf_op jit(solution)/shard_map/ppermute | solution.py:489
  51.0 2.4 %collective-permute-done.5 = f32[1,32,256]{2,1,0:T(8,128)S(1)} collective-permute-done((f32[1,32,256]{2,1,0:T(8,128)S(1)}, f32[1,32,256]{2,1,0:T(8,128)S(1)}, u32[]{:S(2)}, u32[]{:S(2)}) %collective-permute-start.5) | collective-permute-done | bytes 32800 | tf_op jit(solution)/shard_map/ppermute | solution.py:489
  53.3 0.6 collective-permute-start.6
  53.9 2.5 %collective-permute-done.6 = f32[1,32,256]{2,1,0:T(8,128)S(1)} collective-permute-done((f32[1,32,256]{2,1,0:T(8,128)S(1)}, f32[1,32,256]{2,1,0:T(8,128)S(1)}, u32[]{:S(2)}, u32[]{:S(2)}) %collective-permute-start.6) | collective-permute-done | bytes 32800 | tf_op jit(solution)/shard_map/ppermute | solution.py:489
  56.4 2.1 %collective-permute-start.7 = (f32[1,32,256]{2,1,0:T(8,128)S(1)}, f32[1,32,256]{2,1,0:T(8,128)S(1)}, u32[]{:S(2)}, u32[]{:S(2)}) collective-permute-start(f32[1,32,256]{2,1,0:T(8,128)S(1)} %add.45), channel_id=1, source_target_pairs={{0,64},{32,96},{128,192},{160,224},{64,0},{96,32},{192,128},{224,1... | collective-permute-start | bytes 98312 | tf_op jit(solution)/shard_map/ppermute | solution.py:489
  58.5 1.5 %collective-permute-done.7 = f32[1,32,256]{2,1,0:T(8,128)S(1)} collective-permute-done((f32[1,32,256]{2,1,0:T(8,128)S(1)}, f32[1,32,256]{2,1,0:T(8,128)S(1)}, u32[]{:S(2)}, u32[]{:S(2)}) %collective-permute-start.7) | collective-permute-done | bytes 32800 | tf_op jit(solution)/shard_map/ppermute | solution.py:489
  60.1 4.5 %collective-permute-start.8 = (f32[1,32,256]{2,1,0:T(8,128)S(1)}, f32[1,32,256]{2,1,0:T(8,128)S(1)}, u32[]{:S(2)}, u32[]{:S(2)}) collective-permute-start(f32[1,32,256]{2,1,0:T(8,128)S(1)} %add.46), channel_id=1, source_target_pairs={{0,224},{32,192},{64,160},{96,128},{224,0},{192,32},{160,64},{128,... | collective-permute-start | bytes 98312 | tf_op jit(solution)/shard_map/ppermute | solution.py:489
  64.6 0.0 collective-permute-done.9.refs_1_
  64.6 1.1 gram.4.refs_2_
  65.7 0.2 collective-permute-done.8
  65.9 6.0 %collective-permute-done.1.refs_1_.refs_2_ = bf16[1,2,128,1536]{3,2,1,0:T(8,128)(2,1)S(1)} collective-permute-done((bf16[1,2,128,1536]{3,2,1,0:T(8,128)(2,1)S(1)}, bf16[1,2,128,1536]{3,2,1,0:T(8,128)(2,1)S(1)}, u32[]{:S(2)}, u32[]{:S(2)}) %collective-permute-start.1) | collective-permute-done | bytes 786464 | tf_op jit(solution)/shard_map/ppermute | solution.py:504
  71.9 1.1 gram.5
  73.0 2.6 %collective-permute-start.10 = (f32[1,32,256]{2,1,0:T(8,128)S(1)}, f32[1,32,256]{2,1,0:T(8,128)S(1)}, u32[]{:S(2)}, u32[]{:S(2)}) collective-permute-start(f32[1,32,256]{2,1,0:T(8,128)S(1)} %get-tuple-element.29), channel_id=1, source_target_pairs={{0,2},{2,0},{1,3},{3,1},{4,6},{6,4},{5,7},{7,5},{8,10},{10,8},{9,1... | collective-permute-start | bytes 98312 | tf_op jit(solution)/shard_map/ppermute | solution.py:505
  75.7 0.9 collective-permute-done.10
  76.5 1.6 %collective-permute-start.11 = (f32[1,32,256]{2,1,0:T(8,128)S(1)}, f32[1,32,256]{2,1,0:T(8,128)S(1)}, u32[]{:S(2)}, u32[]{:S(2)}) collective-permute-start(f32[1,32,256]{2,1,0:T(8,128)S(1)} %add.48), channel_id=1, source_target_pairs={{0,8},{16,24},{8,0},{24,16},{1,9},{17,25},{9,1},{25,17},{2,10},{18... | collective-permute-start | bytes 98312 | tf_op jit(solution)/shard_map/ppermute | solution.py:489
  78.1 2.7 %collective-permute-start.14 = (f32[1,32,256]{2,1,0:T(8,128)S(1)}, f32[1,32,256]{2,1,0:T(8,128)S(1)}, u32[]{:S(2)}, u32[]{:S(2)}) collective-permute-start(f32[1,32,256]{2,1,0:T(8,128)S(1)} %add.47), channel_id=1, source_target_pairs={{0,4},{4,0},{1,5},{5,1},{2,6},{6,2},{3,7},{7,3},{8,12},{12,8},{9,1... | collective-permute-start | bytes 98312 | tf_op jit(solution)/shard_map/ppermute | solution.py:489
  80.8 0.0 collective-permute-done.11
  80.8 2.2 %collective-permute-start.12 = (f32[1,32,256]{2,1,0:T(8,128)S(1)}, f32[1,32,256]{2,1,0:T(8,128)S(1)}, u32[]{:S(2)}, u32[]{:S(2)}) collective-permute-start(f32[1,32,256]{2,1,0:T(8,128)S(1)} %add.49), channel_id=1, source_target_pairs={{0,24},{8,16},{24,0},{16,8},{1,25},{9,17},{25,1},{17,9},{2,26},{10... | collective-permute-start | bytes 98312 | tf_op jit(solution)/shard_map/ppermute | solution.py:489
  83.0 0.0 collective-permute-done.14
  83.0 2.1 %collective-permute-done.12 = f32[1,32,256]{2,1,0:T(8,128)S(1)} collective-permute-done((f32[1,32,256]{2,1,0:T(8,128)S(1)}, f32[1,32,256]{2,1,0:T(8,128)S(1)}, u32[]{:S(2)}, u32[]{:S(2)}) %collective-permute-start.12) | collective-permute-done | bytes 32800 | tf_op jit(solution)/shard_map/ppermute | solution.py:489
  85.1 1.6 %collective-permute-start.13 = (f32[1,32,256]{2,1,0:T(8,128)S(1)}, f32[1,32,256]{2,1,0:T(8,128)S(1)}, u32[]{:S(2)}, u32[]{:S(2)}) collective-permute-start(f32[1,32,256]{2,1,0:T(8,128)S(1)} %add.50), channel_id=1, source_target_pairs={{0,32},{64,96},{128,160},{192,224},{32,0},{96,64},{160,128},{224,1... | collective-permute-start | bytes 98312 | tf_op jit(solution)/shard_map/ppermute | solution.py:489
  86.7 1.7 %factor.2.full_ref.refs_3_ = f32[72,256]{1,0:T(8,128)S(1)} custom-call(f32[1,32,256]{2,1,0:T(8,128)S(1)} %add.52.sums_ref), custom_call_target="tpu_custom_call" | custom-call | flops 1073741824 | bytes 4194304 | tf_op jit(solution)/shard_map/factor/pallas_call | solution.py:338
  88.4 0.0 collective-permute-done.13
  88.4 3.1 %collective-permute-start.15 = (f32[1,32,256]{2,1,0:T(8,128)S(1)}, f32[1,32,256]{2,1,0:T(8,128)S(1)}, u32[]{:S(2)}, u32[]{:S(2)}) collective-permute-start(f32[1,32,256]{2,1,0:T(8,128)S(1)} %add.51), channel_id=1, source_target_pairs={{0,64},{32,96},{128,192},{160,224},{64,0},{96,32},{192,128},{224,1... | collective-permute-start | bytes 98312 | tf_op jit(solution)/shard_map/ppermute | solution.py:489
  91.5 2.9 %collective-permute-start.19 = (f32[72,256]{1,0:T(8,128)S(1)}, f32[72,256]{1,0:T(8,128)S(1)}, u32[]{:S(2)}, u32[]{:S(2)}) collective-permute-start(f32[72,256]{1,0:T(8,128)S(1)} %factor.2.full_ref.refs_3_), channel_id=1, source_target_pairs={{0,2},{2,0},{1,3},{3,1},{4,6},{6,4},{5,7},{7,5},{8,10},{10,8},{9,1... | collective-permute-start | bytes 221192 | tf_op jit(solution)/shard_map/ppermute | solution.py:505
  94.3 0.0 collective-permute-done.15
  94.4 3.8 %collective-permute-start.16 = (f32[1,32,256]{2,1,0:T(8,128)S(1)}, f32[1,32,256]{2,1,0:T(8,128)S(1)}, u32[]{:S(2)}, u32[]{:S(2)}) collective-permute-start(f32[1,32,256]{2,1,0:T(8,128)S(1)} %add.53), channel_id=1, source_target_pairs={{0,224},{32,192},{64,160},{96,128},{224,0},{192,32},{160,64},{128,... | collective-permute-start | bytes 98312 | tf_op jit(solution)/shard_map/ppermute | solution.py:489
  98.2 3.0 %apply.4.refs_3_ = bf16[32,2,32,1536]{3,2,1,0:T(8,128)(2,1)} custom-call(s32[1]{0:T(128)} %bitcast.owner_ref, s32[1]{0:T(128)} %bitcast.1.core_ref, f32[72,256]{1,0:T(8,128)S(1)} %factor.2.full_ref.refs_3_, bf16[2,2,128,1536]{3,2,1,0:T(8,128)(2,1)S(1)} %bitcast.13, bf16[2,2,32,1536]{3,2,1,0:T(8,128)(2,1)S(1)} %collective-permute-done.refs_1_, ...), custom_call_target="tpu_custom_call" | custom-call | flops 1610612736 | bytes 4194304 | tf_op jit(solution)/shard_map/apply/pallas_call | solution.py:448
  101.2 0.0 collective-permute-done.19.full_ref.refs_4_
  101.2 0.0 collective-permute-done.16
  101.2 1.9 %collective-permute-start.17 = (f32[1,32,256]{2,1,0:T(8,128)S(1)}, f32[1,32,256]{2,1,0:T(8,128)S(1)}, u32[]{:S(2)}, u32[]{:S(2)}) collective-permute-start(f32[1,32,256]{2,1,0:T(8,128)S(1)} %add.54), channel_id=1, source_target_pairs={{0,4},{4,0},{1,5},{5,1},{2,6},{6,2},{3,7},{7,3},{8,12},{12,8},{9,1... | collective-permute-start | bytes 98312 | tf_op jit(solution)/shard_map/ppermute | solution.py:489
  103.1 3.0 %apply.5.refs_3_ = bf16[32,2,32,1536]{3,2,1,0:T(8,128)(2,1)} custom-call(s32[1]{0:T(128)} %bitcast.owner_ref, s32[1]{0:T(128)} %bitcast.1.core_ref, f32[72,256]{1,0:T(8,128)S(1)} %collective-permute-done.19.full_ref.refs_4_, bf16[2,2,128,1536]{3,2,1,0:T(8,128)(2,1)S(1)} %bitcast.14, ...), custom_call_target="tpu_custom_call", output_to_operand_aliasing={{}: (6, {})} | custom-call | flops 1610612736 | bytes 4194304 | tf_op jit(solution)/shard_map/apply/pallas_call | solution.py:448
  106.1 0.0 collective-permute-done.17
  106.2 1.7 %factor.3.full_ref.refs_5_ = f32[72,256]{1,0:T(8,128)S(1)} custom-call(f32[1,32,256]{2,1,0:T(8,128)S(1)} %add.55.sums_ref), custom_call_target="tpu_custom_call" | custom-call | flops 1073741824 | bytes 4194304 | tf_op jit(solution)/shard_map/factor/pallas_call | solution.py:338
  107.8 4.5 %collective-permute-start.18 = (f32[72,256]{1,0:T(8,128)S(1)}, f32[72,256]{1,0:T(8,128)S(1)}, u32[]{:S(2)}, u32[]{:S(2)}) collective-permute-start(f32[72,256]{1,0:T(8,128)S(1)} %factor.3.full_ref.refs_5_), channel_id=1, source_target_pairs={{0,2},{2,0},{1,3},{3,1},{4,6},{6,4},{5,7},{7,5},{8,10},{10,8},{9,1... | collective-permute-start | bytes 221192 | tf_op jit(solution)/shard_map/ppermute | solution.py:505
  112.3 3.0 %apply.6.refs_6_ = bf16[32,2,32,1536]{3,2,1,0:T(8,128)(2,1)} custom-call(s32[1]{0:T(128)} %bitcast.owner_ref, s32[1]{0:T(128)} %bitcast.1.core_ref, f32[72,256]{1,0:T(8,128)S(1)} %factor.3.full_ref.refs_5_, bf16[2,2,128,1536]{3,2,1,0:T(8,128)(2,1)S(1)} %bitcast.10, ...), custom_call_target="tpu_custom_call", output_to_operand_aliasing={{}: (6, {})} | custom-call | flops 1610612736 | bytes 4194304 | tf_op jit(solution)/shard_map/apply/pallas_call | solution.py:448
  115.3 0.0 collective-permute-done.18.full_ref
  115.3 3.0 %apply.7 = (bf16[32,2,32,1536]{3,2,1,0:T(8,128)(2,1)}, f32[32,64]{1,0:T(8,128)}) custom-call(s32[1]{0:T(128)} %bitcast.owner_ref, s32[1]{0:T(128)} %bitcast.1.core_ref, f32[72,256]{1,0:T(8,128)S(1)} %collective-permute-done.18.full_ref, bf16[2,2,128,1536]{3,2,1,0:T(8,128)(2,1)S(1)} %bitcast.11, ...), custom_call_target="tpu_custom_call", output_to_operand_aliasing={{0}: (9, {})} | custom-call | flops 1610612736 | bytes 4194304 | tf_op jit(solution)/shard_map/apply/pallas_call | solution.py:448
  (15 shorter events, 0.1 us)
Async XLA Ops:
  3.1 6.6 %copy-start.2 = (f32[1536]{0:T(1024)S(1)}, f32[1536]{0:T(1024)}, u32[]{:S(2)}) copy-start(f32[1536]{0:T(1024)} %param.6) | copy-start | bytes 18436
  3.1 10.0 %copy-start.1 = (bf16[2,192,256]{2,1,0:T(8,128)(2,1)S(1)}, bf16[2,192,256]{2,1,0:T(8,128)(2,1)}, u32[]{:S(2)}) copy-start(bf16[2,192,256]{2,1,0:T(8,128)(2,1)} %constant.11.clone.table_ref) | copy-start | bytes 589828
  3.1 9.9 %collective-permute-start = (bf16[2,2,32,1536]{3,2,1,0:T(8,128)(2,1)}, bf16[2,2,32,1536]{3,2,1,0:T(8,128)(2,1)S(1)}, u32[]{:S(2)}, u32[]{:S(2)}) collective-permute-start(bf16[2,2,32,1536]{3,2,1,0:T(8,128)(2,1)} %bitcast.18), channel_id=1, source_target_pairs={{0,1},{1,0},{2,3},{3,2},{4,5},{5,4},{6,7},{7,6},{8,9},{9,8},{10,11... | collective-permute-start | bytes 1179656 | tf_op jit(solution)/shard_map/ppermute | solution.py:504
  9.5 28.8 %collective-permute-start.2 = (bf16[2,2,96,1536]{3,2,1,0:T(8,128)(2,1)}, bf16[2,2,96,1536]{3,2,1,0:T(8,128)(2,1)S(1)}, u32[]{:S(2)}, u32[]{:S(2)}) collective-permute-start(bf16[2,2,96,1536]{3,2,1,0:T(8,128)(2,1)} %bitcast.17), channel_id=1, source_target_pairs={{0,1},{1,0},{2,3},{3,2},{4,5},{5,4},{6,7},{7,6},{8,9},{9,8},{10,11... | collective-permute-start | bytes 3538952 | tf_op jit(solution)/shard_map/ppermute | solution.py:504
  13.0 2.8 %copy-start = (bf16[16,128,1536]{2,1,0:T(8,128)(2,1)S(1)}, bf16[16,128,1536]{2,1,0:T(8,128)(2,1)}, u32[]{:S(2)}) copy-start(bf16[16,128,1536]{2,1,0:T(8,128)(2,1)} %record_ref.3) | copy-start | bytes 18874372
  18.8 45.8 %collective-permute-start.9 = (bf16[1,2,128,1536]{3,2,1,0:T(8,128)(2,1)S(1)}, bf16[1,2,128,1536]{3,2,1,0:T(8,128)(2,1)S(1)}, u32[]{:S(2)}, u32[]{:S(2)}) collective-permute-start(bf16[1,2,128,1536]{3,2,1,0:T(8,128)(2,1)S(1)} %bitcast.16), channel_id=1, source_target_pairs={{0,1},{1,0},{2,3},{3,2},{4,5},{5,4},{6,7},{7,6},{8,9},{9,8},{10,11... | collective-permute-start | bytes 2359304 | tf_op jit(solution)/shard_map/ppermute | solution.py:504
  21.0 50.9 %collective-permute-start.1 = (bf16[1,2,128,1536]{3,2,1,0:T(8,128)(2,1)S(1)}, bf16[1,2,128,1536]{3,2,1,0:T(8,128)(2,1)S(1)}, u32[]{:S(2)}, u32[]{:S(2)}) collective-permute-start(bf16[1,2,128,1536]{3,2,1,0:T(8,128)(2,1)S(1)} %bitcast.15), channel_id=1, source_target_pairs={{0,1},{1,0},{2,3},{3,2},{4,5},{5,4},{6,7},{7,6},{8,9},{9,8},{10,11... | collective-permute-start | bytes 2359304 | tf_op jit(solution)/shard_map/ppermute | solution.py:504
  40.4 5.9 %collective-permute-start.3 = (f32[1,32,256]{2,1,0:T(8,128)S(1)}, f32[1,32,256]{2,1,0:T(8,128)S(1)}, u32[]{:S(2)}, u32[]{:S(2)}) collective-permute-start(f32[1,32,256]{2,1,0:T(8,128)S(1)} %get-tuple-element.24), channel_id=1, source_target_pairs={{0,2},{2,0},{1,3},{3,1},{4,6},{6,4},{5,7},{7,5},{8,10},{10,8},{9,1... | collective-permute-start | bytes 98312 | tf_op jit(solution)/shard_map/ppermute | solution.py:505
  46.3 3.1 %collective-permute-start.4 = (f32[1,32,256]{2,1,0:T(8,128)S(1)}, f32[1,32,256]{2,1,0:T(8,128)S(1)}, u32[]{:S(2)}, u32[]{:S(2)}) collective-permute-start(f32[1,32,256]{2,1,0:T(8,128)S(1)} %add.42), channel_id=1, source_target_pairs={{0,8},{16,24},{8,0},{24,16},{1,9},{17,25},{9,1},{25,17},{2,10},{18... | collective-permute-start | bytes 98312 | tf_op jit(solution)/shard_map/ppermute | solution.py:489
  49.4 4.0 %collective-permute-start.5 = (f32[1,32,256]{2,1,0:T(8,128)S(1)}, f32[1,32,256]{2,1,0:T(8,128)S(1)}, u32[]{:S(2)}, u32[]{:S(2)}) collective-permute-start(f32[1,32,256]{2,1,0:T(8,128)S(1)} %add.43), channel_id=1, source_target_pairs={{0,24},{8,16},{24,0},{16,8},{1,25},{9,17},{25,1},{17,9},{2,26},{10... | collective-permute-start | bytes 98312 | tf_op jit(solution)/shard_map/ppermute | solution.py:489
  53.3 3.1 %collective-permute-start.6 = (f32[1,32,256]{2,1,0:T(8,128)S(1)}, f32[1,32,256]{2,1,0:T(8,128)S(1)}, u32[]{:S(2)}, u32[]{:S(2)}) collective-permute-start(f32[1,32,256]{2,1,0:T(8,128)S(1)} %add.44), channel_id=1, source_target_pairs={{0,32},{64,96},{128,160},{192,224},{32,0},{96,64},{160,128},{224,1... | collective-permute-start | bytes 98312 | tf_op jit(solution)/shard_map/ppermute | solution.py:489
  56.4 3.7 %collective-permute-start.7 = (f32[1,32,256]{2,1,0:T(8,128)S(1)}, f32[1,32,256]{2,1,0:T(8,128)S(1)}, u32[]{:S(2)}, u32[]{:S(2)}) collective-permute-start(f32[1,32,256]{2,1,0:T(8,128)S(1)} %add.45), channel_id=1, source_target_pairs={{0,64},{32,96},{128,192},{160,224},{64,0},{96,32},{192,128},{224,1... | collective-permute-start | bytes 98312 | tf_op jit(solution)/shard_map/ppermute | solution.py:489
  60.1 5.8 %collective-permute-start.8 = (f32[1,32,256]{2,1,0:T(8,128)S(1)}, f32[1,32,256]{2,1,0:T(8,128)S(1)}, u32[]{:S(2)}, u32[]{:S(2)}) collective-permute-start(f32[1,32,256]{2,1,0:T(8,128)S(1)} %add.46), channel_id=1, source_target_pairs={{0,224},{32,192},{64,160},{96,128},{224,0},{192,32},{160,64},{128,... | collective-permute-start | bytes 98312 | tf_op jit(solution)/shard_map/ppermute | solution.py:489
  73.0 3.5 %collective-permute-start.10 = (f32[1,32,256]{2,1,0:T(8,128)S(1)}, f32[1,32,256]{2,1,0:T(8,128)S(1)}, u32[]{:S(2)}, u32[]{:S(2)}) collective-permute-start(f32[1,32,256]{2,1,0:T(8,128)S(1)} %get-tuple-element.29), channel_id=1, source_target_pairs={{0,2},{2,0},{1,3},{3,1},{4,6},{6,4},{5,7},{7,5},{8,10},{10,8},{9,1... | collective-permute-start | bytes 98312 | tf_op jit(solution)/shard_map/ppermute | solution.py:505
  76.5 4.3 %collective-permute-start.11 = (f32[1,32,256]{2,1,0:T(8,128)S(1)}, f32[1,32,256]{2,1,0:T(8,128)S(1)}, u32[]{:S(2)}, u32[]{:S(2)}) collective-permute-start(f32[1,32,256]{2,1,0:T(8,128)S(1)} %add.48), channel_id=1, source_target_pairs={{0,8},{16,24},{8,0},{24,16},{1,9},{17,25},{9,1},{25,17},{2,10},{18... | collective-permute-start | bytes 98312 | tf_op jit(solution)/shard_map/ppermute | solution.py:489
  78.1 4.9 %collective-permute-start.14 = (f32[1,32,256]{2,1,0:T(8,128)S(1)}, f32[1,32,256]{2,1,0:T(8,128)S(1)}, u32[]{:S(2)}, u32[]{:S(2)}) collective-permute-start(f32[1,32,256]{2,1,0:T(8,128)S(1)} %add.47), channel_id=1, source_target_pairs={{0,4},{4,0},{1,5},{5,1},{2,6},{6,2},{3,7},{7,3},{8,12},{12,8},{9,1... | collective-permute-start | bytes 98312 | tf_op jit(solution)/shard_map/ppermute | solution.py:489
  80.8 4.2 %collective-permute-start.12 = (f32[1,32,256]{2,1,0:T(8,128)S(1)}, f32[1,32,256]{2,1,0:T(8,128)S(1)}, u32[]{:S(2)}, u32[]{:S(2)}) collective-permute-start(f32[1,32,256]{2,1,0:T(8,128)S(1)} %add.49), channel_id=1, source_target_pairs={{0,24},{8,16},{24,0},{16,8},{1,25},{9,17},{25,1},{17,9},{2,26},{10... | collective-permute-start | bytes 98312 | tf_op jit(solution)/shard_map/ppermute | solution.py:489
  85.1 3.3 %collective-permute-start.13 = (f32[1,32,256]{2,1,0:T(8,128)S(1)}, f32[1,32,256]{2,1,0:T(8,128)S(1)}, u32[]{:S(2)}, u32[]{:S(2)}) collective-permute-start(f32[1,32,256]{2,1,0:T(8,128)S(1)} %add.50), channel_id=1, source_target_pairs={{0,32},{64,96},{128,160},{192,224},{32,0},{96,64},{160,128},{224,1... | collective-permute-start | bytes 98312 | tf_op jit(solution)/shard_map/ppermute | solution.py:489
  88.4 5.9 %collective-permute-start.15 = (f32[1,32,256]{2,1,0:T(8,128)S(1)}, f32[1,32,256]{2,1,0:T(8,128)S(1)}, u32[]{:S(2)}, u32[]{:S(2)}) collective-permute-start(f32[1,32,256]{2,1,0:T(8,128)S(1)} %add.51), channel_id=1, source_target_pairs={{0,64},{32,96},{128,192},{160,224},{64,0},{96,32},{192,128},{224,1... | collective-permute-start | bytes 98312 | tf_op jit(solution)/shard_map/ppermute | solution.py:489
  91.5 9.7 %collective-permute-start.19 = (f32[72,256]{1,0:T(8,128)S(1)}, f32[72,256]{1,0:T(8,128)S(1)}, u32[]{:S(2)}, u32[]{:S(2)}) collective-permute-start(f32[72,256]{1,0:T(8,128)S(1)} %factor.2.full_ref.refs_3_), channel_id=1, source_target_pairs={{0,2},{2,0},{1,3},{3,1},{4,6},{6,4},{5,7},{7,5},{8,10},{10,8},{9,1... | collective-permute-start | bytes 221192 | tf_op jit(solution)/shard_map/ppermute | solution.py:505
  94.4 6.9 %collective-permute-start.16 = (f32[1,32,256]{2,1,0:T(8,128)S(1)}, f32[1,32,256]{2,1,0:T(8,128)S(1)}, u32[]{:S(2)}, u32[]{:S(2)}) collective-permute-start(f32[1,32,256]{2,1,0:T(8,128)S(1)} %add.53), channel_id=1, source_target_pairs={{0,224},{32,192},{64,160},{96,128},{224,0},{192,32},{160,64},{128,... | collective-permute-start | bytes 98312 | tf_op jit(solution)/shard_map/ppermute | solution.py:489
  101.2 4.9 %collective-permute-start.17 = (f32[1,32,256]{2,1,0:T(8,128)S(1)}, f32[1,32,256]{2,1,0:T(8,128)S(1)}, u32[]{:S(2)}, u32[]{:S(2)}) collective-permute-start(f32[1,32,256]{2,1,0:T(8,128)S(1)} %add.54), channel_id=1, source_target_pairs={{0,4},{4,0},{1,5},{5,1},{2,6},{6,2},{3,7},{7,3},{8,12},{12,8},{9,1... | collective-permute-start | bytes 98312 | tf_op jit(solution)/shard_map/ppermute | solution.py:489
  107.8 7.5 %collective-permute-start.18 = (f32[72,256]{1,0:T(8,128)S(1)}, f32[72,256]{1,0:T(8,128)S(1)}, u32[]{:S(2)}, u32[]{:S(2)}) collective-permute-start(f32[72,256]{1,0:T(8,128)S(1)} %factor.3.full_ref.refs_5_), channel_id=1, source_target_pairs={{0,2},{2,0},{1,3},{3,1},{4,6},{6,4},{5,7},{7,5},{8,10},{10,8},{9,1... | collective-permute-start | bytes 221192 | tf_op jit(solution)/shard_map/ppermute | solution.py:505

commit v3 on v2

--- a/solution.py
+++ b/solution.py
@@ -351,25 +351,24 @@
     lane = lax.broadcasted_iota(jnp.int32, (256, 256), 1)
     same = out_row // 32 == lane % 8
     order = (same & (out_row % 32 == lane // 8)).astype(jnp.bfloat16)
-    b_row = lax.broadcasted_iota(jnp.int32, (32, 256), 0)
-    b_lane = lax.broadcasted_iota(jnp.int32, (32, 256), 1) // 8
-    spread = (b_row == (b_lane + 16 * owner) % 32).astype(jnp.bfloat16)
     high = full.astype(jnp.bfloat16)
     low = (full - high.astype(jnp.float32)).astype(jnp.bfloat16)
-    for level, value in enumerate((high, low)):
-        rows = nt_dot(order, value).astype(jnp.bfloat16)
-        for c in range(2):
-            wide = jnp.dot(
-                rows[:, 32 * c : 32 * c + 32], spread, preferred_element_type=jnp.float32
-            )
-            wide = jnp.where(same, wide, 0.0)
-            at = 256 * (2 * c + level)
-            maps_ref[0, :, at : at + 256] = (wide if c == 0 else -wide).astype(jnp.bfloat16)
-            at = 256 * (2 * (1 - c) + level)
-            maps_ref[1, :, at : at + 256] = wide.astype(jnp.bfloat16)
-
-
-def apply_kernel(base, theirs, plan, energies, owner_ref, core_ref, full_ref, *refs):
+    both = jnp.concatenate([high, low], axis=0)
+    rows = nt_dot(order, both).astype(jnp.bfloat16)
+    from_row = lax.broadcasted_iota(jnp.int32, (128, 1024), 0)
+    to_lane = lax.broadcasted_iota(jnp.int32, (128, 1024), 1)
+    b_lane = (to_lane % 256 // 8 + 16 * owner) % 32
+    level, c = to_lane // 256 % 2, to_lane // 512
+    spread = (from_row == 64 * level + 32 * c + b_lane).astype(jnp.bfloat16)
+    wide = jnp.dot(rows, spread, preferred_element_type=jnp.float32)
+    for at in range(0, 1024, 256):
+        part = jnp.where(same, wide[:, at : at + 256], 0.0)
+        maps_ref[0, :, at : at + 256] = (part if at < 512 else -part).astype(jnp.bfloat16)
+        swapped = (at + 512) % 1024
+        maps_ref[1, :, swapped : swapped + 256] = part.astype(jnp.bfloat16)
+
+
+def apply_kernel(base, theirs, plan, column, energies, owner_ref, core_ref, full_ref, *refs):
     count = max(ref for parts in plan for ref, _ in parts) + 1
     rows, refs = refs[:count], refs[count:]
     if energies:
@@ -396,13 +395,14 @@
     for part in range(sems.shape[0]):
         for start in range(part * piece, (part + 1) * piece, width):
             cols = pl.ds(start, width)
+            read = pl.ds(column + start, width)
             x0, x1 = (
                 jnp.concatenate(
                     [
-                        rows[ref][chosen, c, :, cols]
+                        rows[ref][chosen, c, :, read]
                         if rows[ref].shape[0] == 2
                         else jnp.where(
-                            chosen == 0, rows[ref][0, c, :, cols], rows[other][0, c, :, cols]
+                            chosen == 0, rows[ref][0, c, :, read], rows[other][0, c, :, read]
                         )
                         for (ref, _), (other, _) in zip(*plan)
                     ],
@@ -416,7 +416,9 @@
                 held_ref[:, c, :, cols] = value.astype(jnp.bfloat16).reshape(8, 32, width)
         cols = pl.ds(part * piece, piece)
         copy = pltpu.make_async_copy(
-            held_ref.at[:, :, :, cols], target.at[:, :, :, cols], sems.at[part]
+            held_ref.at[:, :, :, cols],
+            target.at[:, :, :, pl.ds(column + part * piece, piece)],
+            sems.at[part],
         )
         copy.start()
         copies.append(copy)
@@ -428,9 +430,12 @@
     return jax.ShapeDtypeStruct((8 * total_chunks, 2, 32, points), jnp.bfloat16)
 
 
-def apply_call(place, full, rows, modes, base, theirs, total_chunks, others=()):
+def apply_call(
+    place, full, rows, modes, base, theirs, total_chunks, others=(), column=0, width=None
+):
     arrays, plan = plan_of(rows)
     points = arrays[0].shape[-1]
+    width = width or points
     operands = [*place, full, *arrays, *others]
     in_specs = [pl.BlockSpec(memory_space=pltpu.SMEM)] * 2
     in_specs += [pl.BlockSpec(memory_space=pltpu.VMEM)] * (len(operands) - 2)
@@ -446,20 +451,20 @@
         out_shape.append(jax.ShapeDtypeStruct((8 * total_chunks, 64), jnp.float32))
         small = [pltpu.VMEM((8 * total_chunks, 64), jnp.float32), pltpu.SemaphoreType.DMA]
     return pl.pallas_call(
-        functools.partial(apply_kernel, base, theirs, plan, bool(others)),
+        functools.partial(apply_kernel, base, theirs, plan, column, bool(others)),
         in_specs=in_specs,
         out_specs=out_specs,
         out_shape=out_shape,
         scratch_shapes=small
         + [
             pltpu.VMEM((2, 256, 1024), jnp.bfloat16),
-            pltpu.VMEM((8, 2, 32, points), jnp.bfloat16),
-            pltpu.SemaphoreType.DMA((6,)),
+            pltpu.VMEM((8, 2, 32, width), jnp.bfloat16),
+            pltpu.SemaphoreType.DMA((width // 256,)),
         ],
         input_output_aliases=aliases,
         compiler_params=pltpu.CompilerParams(vmem_limit_bytes=16 * MIB),
         cost_estimate=pl.CostEstimate(
-            flops=16 * 256 * 256 * points, bytes_accessed=4 * MIB, transcendentals=0
+            flops=16 * 256 * 256 * width, bytes_accessed=2 * MIB, transcendentals=0
         ),
         name="apply",
     )(*operands)
@@ -528,18 +533,22 @@
     peer_d = after(peer_d, ab)
     cd, other = gram([[(own_cd, 1), (peer_d, 0)]], c)
     rows_cd = [[(own_cd, 0), (peer_c, 0)], [(own_cd, 1), (peer_d, 0)]]
-    ab = add_step(ab, STEPS[5])
     cd = cd + cross(other)
+    ab = add_step(after(ab, cd), STEPS[5])
     cd = add_step(cd, STEPS[0])
     mine_ab = factor_call(after(ab, cd), points * space)
     theirs_ab = cross(mine_ab)
-    for step in STEPS[1:3]:
-        cd = add_step(cd, step)
-    modes = apply(after(mine_ab, cd), rows_ab, None, 0, False)[0]
-    cd = add_step(after(cd, mine_ab), STEPS[3])
-    modes = apply(after(theirs_ab, cd), rows_ab, modes, 0, True)[0]
-    for step in STEPS[4:]:
-        cd = add_step(cd, step)
+    half, modes = points // 2, None
+    for step, theirs, column in (
+        (1, False, 0),
+        (2, False, half),
+        (3, True, 0),
+        (4, True, half),
+    ):
+        cd = add_step(cd, STEPS[step])
+        full = after(theirs_ab if theirs else mine_ab, cd)
+        modes = apply(full, rows_ab, modes, 0, theirs, column=column, width=half)[0]
+    cd = add_step(cd, STEPS[5])
     mine_cd = factor_call(cd, points * space)
     theirs_cd = cross(mine_cd)
     modes = apply(mine_cd, rows_cd, modes, 2, False)[0]

time: 119 us -> 118 us (level)
  Pallas kernels: 29.3 us -> 31.3 us
  waiting for transfers between devices: 39.8 us -> 37.8 us
    ppermute x12, waiting for transfers between devices: 11.5 us -> 9.46 us  [add_step(): return value + lax.ppermute(value, axis, pairs)]
    pallas_call x4 -> x6, Pallas kernels: 12.1 us -> 14.1 us  [apply_call(): pl.pallas_call(functools.partial(apply_kernel, base, theirs, plan, column...]
    ppermute x4, starting transfers between devices: 15 us -> 13.6 us  [local(): cross = lambda value: lax.ppermute(value, *CORE)]
  transfers between devices with their start and end apart: 20 -> 20, of which waited for: 11 -> 10; matrix products, arithmetic and copies ran while one was open for 0% -> 0% of each run, Pallas kernels for 18% -> 20%
where the time goes in v3:
time: 118 us; the launch traced here: 117 us
  starting transfers between devices  44.4 us (38%)
  waiting for transfers between devices  37.8 us (32%)
  Pallas kernels  31.3 us (27%)
  local copies, waits for them, and re-layouts  2.8 us (2%)
    ppermute x4, waiting for transfers between devices, local(): swap = lambda s: lax.ppermute(s, 'blk', [(0, 1), (1, 0)])  26.6 us
    ppermute x12, starting transfers between devices, add_step(): return value + lax.ppermute(value, axis, pairs)  26.3 us
    pallas_call x6, Pallas kernels, apply_call(): pl.pallas_call(functools.partial(apply_kernel, base, theirs, plan, column...  14.1 us
    ppermute x4, starting transfers between devices, local(): cross = lambda value: lax.ppermute(value, *CORE)  13.6 us
    ppermute x12, waiting for transfers between devices, add_step(): return value + lax.ppermute(value, axis, pairs)  9.46 us
    pallas_call x2, Pallas kernels, early_call(): pl.pallas_call(functools.partial(early_kernel, first), in_specs=[pl.Block...  6.71 us
    ppermute x4, starting transfers between devices, local(): swap = lambda s: lax.ppermute(s, 'blk', [(0, 1), (1, 0)])  4.51 us
    pallas_call x3, Pallas kernels, gram_call(): pl.pallas_call(functools.partial(gram_kernel, plan, prior is not None), i...  4.28 us
  transfers between devices with their start and end apart: 20, of which 10 were waited for; matrix products, arithmetic and copies ran while one was open for 0% of the time, Pallas kernels for 20%

profile of v3, /device:TPU:1, one launch (start us, length us, event | category | flops | bytes accessed | tf_op | source)
XLA Modules:
  0.0 117.5 jit_solution(6698794158299653001)
XLA Ops:
  0.6 2.4 %early.2 = bf16[2,2,2,16,1536]{4,3,2,1,0:T(8,128)(2,1)} custom-call(s32[1]{0:T(128)} %bitcast.owner_ref, bf16[2,64,256]{2,1,0:T(8,128)(2,1)} %constant.10.clone.tables_ref, bf16[16,128,1536]{2,1,0:T(8,128)(2,1)} %record_ref.3), custom_call_target="tpu_custom_call" | custom-call | flops 20000000000 | bytes 2097152 | tf_op jit(solution)/shard_map/early/pallas_call | solution.py:72
  3.1 0.0 copy-start.2
  3.1 0.0 copy-start.1
  3.1 2.1 %collective-permute-start = (bf16[2,2,32,1536]{3,2,1,0:T(8,128)(2,1)}, bf16[2,2,32,1536]{3,2,1,0:T(8,128)(2,1)S(1)}, u32[]{:S(2)}, u32[]{:S(2)}) collective-permute-start(bf16[2,2,32,1536]{3,2,1,0:T(8,128)(2,1)} %bitcast.20), channel_id=1, source_target_pairs={{0,1},{1,0},{2,3},{3,2},{4,5},{5,4},{6,7},{7,6},{8,9},{9,8},{10,11... | collective-permute-start | bytes 1179656 | tf_op jit(solution)/shard_map/ppermute | solution.py:509
  5.2 4.3 %early.3 = bf16[2,2,6,16,1536]{4,3,2,1,0:T(8,128)(2,1)} custom-call(s32[1]{0:T(128)} %bitcast.owner_ref, bf16[2,64,256]{2,1,0:T(8,128)(2,1)} %constant.10.clone.tables_ref, bf16[16,128,1536]{2,1,0:T(8,128)(2,1)} %record_ref.3), custom_call_target="tpu_custom_call" | custom-call | flops 20000000000 | bytes 6291456 | tf_op jit(solution)/shard_map/early/pallas_call | solution.py:72
  9.5 0.1 collective-permute-start.2
  9.6 0.0 copy-done.2
  9.6 3.4 %collective-permute-done.refs_1_ = bf16[2,2,32,1536]{3,2,1,0:T(8,128)(2,1)S(1)} collective-permute-done((bf16[2,2,32,1536]{3,2,1,0:T(8,128)(2,1)}, bf16[2,2,32,1536]{3,2,1,0:T(8,128)(2,1)S(1)}, u32[]{:S(2)}, u32[]{:S(2)}) %collective-permute-start) | collective-permute-done | bytes 393248 | tf_op jit(solution)/shard_map/ppermute | solution.py:509
  13.0 0.0 copy-done.1
  13.0 0.0 copy-start
  13.0 2.8 %copy-done = bf16[16,128,1536]{2,1,0:T(8,128)(2,1)S(1)} copy-done((bf16[16,128,1536]{2,1,0:T(8,128)(2,1)S(1)}, bf16[16,128,1536]{2,1,0:T(8,128)(2,1)}, u32[]{:S(2)}) %copy-start) | copy-done | bytes 6291480
  15.8 3.0 %spectra.1 = (bf16[1,2,8,16,1536]{4,3,2,1,0:T(8,128)(2,1)S(1)}, bf16[1,2,8,16,1536]{4,3,2,1,0:T(8,128)(2,1)S(1)}, bf16[2,2,8,16,1536]{4,3,2,1,0:T(8,128)(2,1)S(1)}, bf16[2,2,8,16,1536]{4,3,2,1,0:T(8,128)(2,1)S(1)}) custom-call(s32[1]{0:T(128)} %bitcast.owner_ref, bf16[2,192,256]{2,1,0:T(8,128)(2,1)S(1)} %copy-done.1, bf16[16,128,1536]{2,1,0:T(8,128)(2,1)S(1)} %copy-done), custom_call_target="tpu_custom_call" | custom-call | flops 40000000000 | bytes 12582912 | tf_op jit(solution)/shard_map/spectra/pallas_call | solution.py:116
  18.8 2.2 %collective-permute-start.9 = (bf16[1,2,128,1536]{3,2,1,0:T(8,128)(2,1)S(1)}, bf16[1,2,128,1536]{3,2,1,0:T(8,128)(2,1)S(1)}, u32[]{:S(2)}, u32[]{:S(2)}) collective-permute-start(bf16[1,2,128,1536]{3,2,1,0:T(8,128)(2,1)S(1)} %bitcast.18), channel_id=1, source_target_pairs={{0,1},{1,0},{2,3},{3,2},{4,5},{5,4},{6,7},{7,6},{8,9},{9,8},{10,11... | collective-permute-start | bytes 2359304 | tf_op jit(solution)/shard_map/ppermute | solution.py:509
  21.0 0.1 collective-permute-start.1
  21.1 17.2 %collective-permute-done.2.refs_2_ = bf16[2,2,96,1536]{3,2,1,0:T(8,128)(2,1)S(1)} collective-permute-done((bf16[2,2,96,1536]{3,2,1,0:T(8,128)(2,1)}, bf16[2,2,96,1536]{3,2,1,0:T(8,128)(2,1)S(1)}, u32[]{:S(2)}, u32[]{:S(2)}) %collective-permute-start.2) | collective-permute-done | bytes 1179680 | tf_op jit(solution)/shard_map/ppermute | solution.py:509
  38.3 2.1 %gram.3 = (f32[1,32,256]{2,1,0:T(8,128)S(1)}, f32[1,32,256]{2,1,0:T(8,128)S(1)}) custom-call(s32[1]{0:T(128)} %bitcast.owner_ref, s32[1]{0:T(128)} %bitcast.1.core_ref, f32[1,1536]{1,0:T(1,128)S(1)} %reshape.33.weights_ref, bf16[2,2,128,1536]{3,2,1,0:T(8,128)(2,1)S(1)} %bitcast.8, bf16[2,2,32,1536]{3,2,1,0:T(8,128)(2,1)S(1)} %collective-permute-done.refs_1_, ...), custom_call_target="tpu_custom_call" | custom-call | flops 40000000000 | bytes 4194304 | tf_op jit(solution)/shard_map/gram/pallas_call | solution.py:220
  40.4 5.1 %collective-permute-start.3 = (f32[1,32,256]{2,1,0:T(8,128)S(1)}, f32[1,32,256]{2,1,0:T(8,128)S(1)}, u32[]{:S(2)}, u32[]{:S(2)}) collective-permute-start(f32[1,32,256]{2,1,0:T(8,128)S(1)} %get-tuple-element.26), channel_id=1, source_target_pairs={{0,2},{2,0},{1,3},{3,1},{4,6},{6,4},{5,7},{7,5},{8,10},{10,8},{9,1... | collective-permute-start | bytes 98312 | tf_op jit(solution)/shard_map/ppermute | solution.py:510
  45.4 0.9 collective-permute-done.3
  46.3 0.2 collective-permute-start.4
  46.5 2.9 %collective-permute-done.4 = f32[1,32,256]{2,1,0:T(8,128)S(1)} collective-permute-done((f32[1,32,256]{2,1,0:T(8,128)S(1)}, f32[1,32,256]{2,1,0:T(8,128)S(1)}, u32[]{:S(2)}, u32[]{:S(2)}) %collective-permute-start.4) | collective-permute-done | bytes 32800 | tf_op jit(solution)/shard_map/ppermute | solution.py:494
  49.4 1.6 %collective-permute-start.5 = (f32[1,32,256]{2,1,0:T(8,128)S(1)}, f32[1,32,256]{2,1,0:T(8,128)S(1)}, u32[]{:S(2)}, u32[]{:S(2)}) collective-permute-start(f32[1,32,256]{2,1,0:T(8,128)S(1)} %add.43), channel_id=1, source_target_pairs={{0,24},{8,16},{24,0},{16,8},{1,25},{9,17},{25,1},{17,9},{2,26},{10... | collective-permute-start | bytes 98312 | tf_op jit(solution)/shard_map/ppermute | solution.py:494
  51.0 2.4 %collective-permute-done.5 = f32[1,32,256]{2,1,0:T(8,128)S(1)} collective-permute-done((f32[1,32,256]{2,1,0:T(8,128)S(1)}, f32[1,32,256]{2,1,0:T(8,128)S(1)}, u32[]{:S(2)}, u32[]{:S(2)}) %collective-permute-start.5) | collective-permute-done | bytes 32800 | tf_op jit(solution)/shard_map/ppermute | solution.py:494
  53.3 0.6 collective-permute-start.6
  53.9 2.5 %collective-permute-done.6 = f32[1,32,256]{2,1,0:T(8,128)S(1)} collective-permute-done((f32[1,32,256]{2,1,0:T(8,128)S(1)}, f32[1,32,256]{2,1,0:T(8,128)S(1)}, u32[]{:S(2)}, u32[]{:S(2)}) %collective-permute-start.6) | collective-permute-done | bytes 32800 | tf_op jit(solution)/shard_map/ppermute | solution.py:494
  56.4 2.1 %collective-permute-start.7 = (f32[1,32,256]{2,1,0:T(8,128)S(1)}, f32[1,32,256]{2,1,0:T(8,128)S(1)}, u32[]{:S(2)}, u32[]{:S(2)}) collective-permute-start(f32[1,32,256]{2,1,0:T(8,128)S(1)} %add.45), channel_id=1, source_target_pairs={{0,64},{32,96},{128,192},{160,224},{64,0},{96,32},{192,128},{224,1... | collective-permute-start | bytes 98312 | tf_op jit(solution)/shard_map/ppermute | solution.py:494
  58.5 1.5 %collective-permute-done.7 = f32[1,32,256]{2,1,0:T(8,128)S(1)} collective-permute-done((f32[1,32,256]{2,1,0:T(8,128)S(1)}, f32[1,32,256]{2,1,0:T(8,128)S(1)}, u32[]{:S(2)}, u32[]{:S(2)}) %collective-permute-start.7) | collective-permute-done | bytes 32800 | tf_op jit(solution)/shard_map/ppermute | solution.py:494
  60.1 4.5 %collective-permute-start.8 = (f32[1,32,256]{2,1,0:T(8,128)S(1)}, f32[1,32,256]{2,1,0:T(8,128)S(1)}, u32[]{:S(2)}, u32[]{:S(2)}) collective-permute-start(f32[1,32,256]{2,1,0:T(8,128)S(1)} %add.46), channel_id=1, source_target_pairs={{0,224},{32,192},{64,160},{96,128},{224,0},{192,32},{160,64},{128,... | collective-permute-start | bytes 98312 | tf_op jit(solution)/shard_map/ppermute | solution.py:494
  64.6 0.0 collective-permute-done.9.refs_1_
  64.6 1.1 gram.4.refs_2_
  65.7 0.2 collective-permute-done.8
  65.9 6.0 %collective-permute-done.1.refs_1_.refs_2_ = bf16[1,2,128,1536]{3,2,1,0:T(8,128)(2,1)S(1)} collective-permute-done((bf16[1,2,128,1536]{3,2,1,0:T(8,128)(2,1)S(1)}, bf16[1,2,128,1536]{3,2,1,0:T(8,128)(2,1)S(1)}, u32[]{:S(2)}, u32[]{:S(2)}) %collective-permute-start.1) | collective-permute-done | bytes 786464 | tf_op jit(solution)/shard_map/ppermute | solution.py:509
  71.9 1.1 gram.5
  73.0 2.6 %collective-permute-start.10 = (f32[1,32,256]{2,1,0:T(8,128)S(1)}, f32[1,32,256]{2,1,0:T(8,128)S(1)}, u32[]{:S(2)}, u32[]{:S(2)}) collective-permute-start(f32[1,32,256]{2,1,0:T(8,128)S(1)} %get-tuple-element.31), channel_id=1, source_target_pairs={{0,2},{2,0},{1,3},{3,1},{4,6},{6,4},{5,7},{7,5},{8,10},{10,8},{9,1... | collective-permute-start | bytes 98312 | tf_op jit(solution)/shard_map/ppermute | solution.py:510
  75.7 0.9 collective-permute-done.10
  76.5 1.6 %collective-permute-start.11 = (f32[1,32,256]{2,1,0:T(8,128)S(1)}, f32[1,32,256]{2,1,0:T(8,128)S(1)}, u32[]{:S(2)}, u32[]{:S(2)}) collective-permute-start(f32[1,32,256]{2,1,0:T(8,128)S(1)} %add.48), channel_id=1, source_target_pairs={{0,8},{16,24},{8,0},{24,16},{1,9},{17,25},{9,1},{25,17},{2,10},{18... | collective-permute-start | bytes 98312 | tf_op jit(solution)/shard_map/ppermute | solution.py:494
  78.1 2.7 %collective-permute-start.18 = (f32[1,32,256]{2,1,0:T(8,128)S(1)}, f32[1,32,256]{2,1,0:T(8,128)S(1)}, u32[]{:S(2)}, u32[]{:S(2)}) collective-permute-start(f32[1,32,256]{2,1,0:T(8,128)S(1)} %add.47), channel_id=1, source_target_pairs={{0,4},{4,0},{1,5},{5,1},{2,6},{6,2},{3,7},{7,3},{8,12},{12,8},{9,1... | collective-permute-start | bytes 98312 | tf_op jit(solution)/shard_map/ppermute | solution.py:494
  80.8 0.0 collective-permute-done.11
  80.8 2.2 %collective-permute-start.12 = (f32[1,32,256]{2,1,0:T(8,128)S(1)}, f32[1,32,256]{2,1,0:T(8,128)S(1)}, u32[]{:S(2)}, u32[]{:S(2)}) collective-permute-start(f32[1,32,256]{2,1,0:T(8,128)S(1)} %add.49), channel_id=1, source_target_pairs={{0,24},{8,16},{24,0},{16,8},{1,25},{9,17},{25,1},{17,9},{2,26},{10... | collective-permute-start | bytes 98312 | tf_op jit(solution)/shard_map/ppermute | solution.py:494
  83.0 0.0 collective-permute-done.18
  83.0 1.7 %factor.3.full_ref.refs_3_ = f32[72,256]{1,0:T(8,128)S(1)} custom-call(f32[1,32,256]{2,1,0:T(8,128)S(1)} %add.55.sums_ref), custom_call_target="tpu_custom_call" | custom-call | flops 1073741824 | bytes 4194304 | tf_op jit(solution)/shard_map/factor/pallas_call | solution.py:338
  84.7 1.3 %collective-permute-start.19 = (f32[72,256]{1,0:T(8,128)S(1)}, f32[72,256]{1,0:T(8,128)S(1)}, u32[]{:S(2)}, u32[]{:S(2)}) collective-permute-start(f32[72,256]{1,0:T(8,128)S(1)} %factor.3.full_ref.refs_3_), channel_id=1, source_target_pairs={{0,2},{2,0},{1,3},{3,1},{4,6},{6,4},{5,7},{7,5},{8,10},{10,8},{9,1... | collective-permute-start | bytes 221192 | tf_op jit(solution)/shard_map/ppermute | solution.py:510
  86.0 0.0 collective-permute-done.12
  86.0 1.7 %collective-permute-start.13 = (f32[1,32,256]{2,1,0:T(8,128)S(1)}, f32[1,32,256]{2,1,0:T(8,128)S(1)}, u32[]{:S(2)}, u32[]{:S(2)}) collective-permute-start(f32[1,32,256]{2,1,0:T(8,128)S(1)} %add.50), channel_id=1, source_target_pairs={{0,32},{64,96},{128,160},{192,224},{32,0},{96,64},{160,128},{224,1... | collective-permute-start | bytes 98312 | tf_op jit(solution)/shard_map/ppermute | solution.py:494
  87.7 2.1 %apply.6.refs_3_ = bf16[32,2,32,1536]{3,2,1,0:T(8,128)(2,1)} custom-call(s32[1]{0:T(128)} %bitcast.owner_ref, s32[1]{0:T(128)} %bitcast.1.core_ref, f32[72,256]{1,0:T(8,128)S(1)} %factor.3.full_ref.refs_3_, bf16[2,2,128,1536]{3,2,1,0:T(8,128)(2,1)S(1)} %bitcast.9, bf16[2,2,32,1536]{3,2,1,0:T(8,128)(2,1)S(1)} %collective-permute-done.refs_1_, ...), custom_call_target="tpu_custom_call" | custom-call | flops 805306368 | bytes 2097152 | tf_op jit(solution)/shard_map/apply/pallas_call | solution.py:453
  89.8 0.0 collective-permute-done.13
  89.8 3.1 %collective-permute-start.14 = (f32[1,32,256]{2,1,0:T(8,128)S(1)}, f32[1,32,256]{2,1,0:T(8,128)S(1)}, u32[]{:S(2)}, u32[]{:S(2)}) collective-permute-start(f32[1,32,256]{2,1,0:T(8,128)S(1)} %add.51), channel_id=1, source_target_pairs={{0,64},{32,96},{128,192},{160,224},{64,0},{96,32},{192,128},{224,1... | collective-permute-start | bytes 98312 | tf_op jit(solution)/shard_map/ppermute | solution.py:494
  92.9 2.0 %apply.7.refs_3_ = bf16[32,2,32,1536]{3,2,1,0:T(8,128)(2,1)} custom-call(s32[1]{0:T(128)} %bitcast.owner_ref, s32[1]{0:T(128)} %bitcast.1.core_ref, f32[72,256]{1,0:T(8,128)S(1)} %factor.3.full_ref.refs_3_, bf16[2,2,128,1536]{3,2,1,0:T(8,128)(2,1)S(1)} %bitcast.10, ...), custom_call_target="tpu_custom_call", output_to_operand_aliasing={{}: (6, {})} | custom-call | flops 805306368 | bytes 2097152 | tf_op jit(solution)/shard_map/apply/pallas_call | solution.py:453
  94.9 0.0 collective-permute-done.14
  95.0 3.3 %collective-permute-start.15 = (f32[1,32,256]{2,1,0:T(8,128)S(1)}, f32[1,32,256]{2,1,0:T(8,128)S(1)}, u32[]{:S(2)}, u32[]{:S(2)}) collective-permute-start(f32[1,32,256]{2,1,0:T(8,128)S(1)} %add.52), channel_id=1, source_target_pairs={{0,224},{32,192},{64,160},{96,128},{224,0},{192,32},{160,64},{128,... | collective-permute-start | bytes 98312 | tf_op jit(solution)/shard_map/ppermute | solution.py:494
  98.2 0.0 collective-permute-done.19.full_ref.refs_4_
  98.2 2.1 %apply.8.refs_3_ = bf16[32,2,32,1536]{3,2,1,0:T(8,128)(2,1)} custom-call(s32[1]{0:T(128)} %bitcast.owner_ref, s32[1]{0:T(128)} %bitcast.1.core_ref, f32[72,256]{1,0:T(8,128)S(1)} %collective-permute-done.19.full_ref.refs_4_, bf16[2,2,128,1536]{3,2,1,0:T(8,128)(2,1)S(1)} %bitcast.11, ...), custom_call_target="tpu_custom_call", output_to_operand_aliasing={{}: (6, {})} | custom-call | flops 805306368 | bytes 2097152 | tf_op jit(solution)/shard_map/apply/pallas_call | solution.py:453
  100.3 0.0 collective-permute-done.15
  100.3 2.7 %collective-permute-start.16 = (f32[1,32,256]{2,1,0:T(8,128)S(1)}, f32[1,32,256]{2,1,0:T(8,128)S(1)}, u32[]{:S(2)}, u32[]{:S(2)}) collective-permute-start(f32[1,32,256]{2,1,0:T(8,128)S(1)} %add.53), channel_id=1, source_target_pairs={{0,4},{4,0},{1,5},{5,1},{2,6},{6,2},{3,7},{7,3},{8,12},{12,8},{9,1... | collective-permute-start | bytes 98312 | tf_op jit(solution)/shard_map/ppermute | solution.py:494
  103.1 2.0 %apply.9.refs_3_ = bf16[32,2,32,1536]{3,2,1,0:T(8,128)(2,1)} custom-call(s32[1]{0:T(128)} %bitcast.owner_ref, s32[1]{0:T(128)} %bitcast.1.core_ref, f32[72,256]{1,0:T(8,128)S(1)} %collective-permute-done.19.full_ref.refs_4_, bf16[2,2,128,1536]{3,2,1,0:T(8,128)(2,1)S(1)} %bitcast.12, ...), custom_call_target="tpu_custom_call", output_to_operand_aliasing={{}: (6, {})} | custom-call | flops 805306368 | bytes 2097152 | tf_op jit(solution)/shard_map/apply/pallas_call | solution.py:453
  105.1 0.0 collective-permute-done.16
  105.1 1.7 %factor.2.full_ref.refs_5_ = f32[72,256]{1,0:T(8,128)S(1)} custom-call(f32[1,32,256]{2,1,0:T(8,128)S(1)} %add.54.sums_ref), custom_call_target="tpu_custom_call" | custom-call | flops 1073741824 | bytes 4194304 | tf_op jit(solution)/shard_map/factor/pallas_call | solution.py:338
  106.8 4.6 %collective-permute-start.17 = (f32[72,256]{1,0:T(8,128)S(1)}, f32[72,256]{1,0:T(8,128)S(1)}, u32[]{:S(2)}, u32[]{:S(2)}) collective-permute-start(f32[72,256]{1,0:T(8,128)S(1)} %factor.2.full_ref.refs_5_), channel_id=1, source_target_pairs={{0,2},{2,0},{1,3},{3,1},{4,6},{6,4},{5,7},{7,5},{8,10},{10,8},{9,1... | collective-permute-start | bytes 221192 | tf_op jit(solution)/shard_map/ppermute | solution.py:510
  111.4 2.9 %apply.10.refs_6_ = bf16[32,2,32,1536]{3,2,1,0:T(8,128)(2,1)} custom-call(s32[1]{0:T(128)} %bitcast.owner_ref, s32[1]{0:T(128)} %bitcast.1.core_ref, f32[72,256]{1,0:T(8,128)S(1)} %factor.2.full_ref.refs_5_, bf16[2,2,128,1536]{3,2,1,0:T(8,128)(2,1)S(1)} %bitcast.15, ...), custom_call_target="tpu_custom_call", output_to_operand_aliasing={{}: (6, {})} | custom-call | flops 1610612736 | bytes 2097152 | tf_op jit(solution)/shard_map/apply/pallas_call | solution.py:453
  114.4 0.0 collective-permute-done.17.full_ref
  114.4 2.9 %apply.11 = (bf16[32,2,32,1536]{3,2,1,0:T(8,128)(2,1)}, f32[32,64]{1,0:T(8,128)}) custom-call(s32[1]{0:T(128)} %bitcast.owner_ref, s32[1]{0:T(128)} %bitcast.1.core_ref, f32[72,256]{1,0:T(8,128)S(1)} %collective-permute-done.17.full_ref, bf16[2,2,128,1536]{3,2,1,0:T(8,128)(2,1)S(1)} %bitcast.16, ...), custom_call_target="tpu_custom_call", output_to_operand_aliasing={{0}: (9, {})} | custom-call | flops 1610612736 | bytes 2097152 | tf_op jit(solution)/shard_map/apply/pallas_call | solution.py:453
  (15 shorter events, 0.1 us)
Async XLA Ops:
  3.1 6.6 %copy-start.2 = (f32[1536]{0:T(1024)S(1)}, f32[1536]{0:T(1024)}, u32[]{:S(2)}) copy-start(f32[1536]{0:T(1024)} %param.6) | copy-start | bytes 18436
  3.1 10.0 %copy-start.1 = (bf16[2,192,256]{2,1,0:T(8,128)(2,1)S(1)}, bf16[2,192,256]{2,1,0:T(8,128)(2,1)}, u32[]{:S(2)}) copy-start(bf16[2,192,256]{2,1,0:T(8,128)(2,1)} %constant.11.clone.table_ref) | copy-start | bytes 589828
  3.1 9.9 %collective-permute-start = (bf16[2,2,32,1536]{3,2,1,0:T(8,128)(2,1)}, bf16[2,2,32,1536]{3,2,1,0:T(8,128)(2,1)S(1)}, u32[]{:S(2)}, u32[]{:S(2)}) collective-permute-start(bf16[2,2,32,1536]{3,2,1,0:T(8,128)(2,1)} %bitcast.20), channel_id=1, source_target_pairs={{0,1},{1,0},{2,3},{3,2},{4,5},{5,4},{6,7},{7,6},{8,9},{9,8},{10,11... | collective-permute-start | bytes 1179656 | tf_op jit(solution)/shard_map/ppermute | solution.py:509
  9.5 28.8 %collective-permute-start.2 = (bf16[2,2,96,1536]{3,2,1,0:T(8,128)(2,1)}, bf16[2,2,96,1536]{3,2,1,0:T(8,128)(2,1)S(1)}, u32[]{:S(2)}, u32[]{:S(2)}) collective-permute-start(bf16[2,2,96,1536]{3,2,1,0:T(8,128)(2,1)} %bitcast.19), channel_id=1, source_target_pairs={{0,1},{1,0},{2,3},{3,2},{4,5},{5,4},{6,7},{7,6},{8,9},{9,8},{10,11... | collective-permute-start | bytes 3538952 | tf_op jit(solution)/shard_map/ppermute | solution.py:509
  13.0 2.8 %copy-start = (bf16[16,128,1536]{2,1,0:T(8,128)(2,1)S(1)}, bf16[16,128,1536]{2,1,0:T(8,128)(2,1)}, u32[]{:S(2)}) copy-start(bf16[16,128,1536]{2,1,0:T(8,128)(2,1)} %record_ref.3) | copy-start | bytes 18874372
  18.8 45.8 %collective-permute-start.9 = (bf16[1,2,128,1536]{3,2,1,0:T(8,128)(2,1)S(1)}, bf16[1,2,128,1536]{3,2,1,0:T(8,128)(2,1)S(1)}, u32[]{:S(2)}, u32[]{:S(2)}) collective-permute-start(bf16[1,2,128,1536]{3,2,1,0:T(8,128)(2,1)S(1)} %bitcast.18), channel_id=1, source_target_pairs={{0,1},{1,0},{2,3},{3,2},{4,5},{5,4},{6,7},{7,6},{8,9},{9,8},{10,11... | collective-permute-start | bytes 2359304 | tf_op jit(solution)/shard_map/ppermute | solution.py:509
  21.0 50.9 %collective-permute-start.1 = (bf16[1,2,128,1536]{3,2,1,0:T(8,128)(2,1)S(1)}, bf16[1,2,128,1536]{3,2,1,0:T(8,128)(2,1)S(1)}, u32[]{:S(2)}, u32[]{:S(2)}) collective-permute-start(bf16[1,2,128,1536]{3,2,1,0:T(8,128)(2,1)S(1)} %bitcast.17), channel_id=1, source_target_pairs={{0,1},{1,0},{2,3},{3,2},{4,5},{5,4},{6,7},{7,6},{8,9},{9,8},{10,11... | collective-permute-start | bytes 2359304 | tf_op jit(solution)/shard_map/ppermute | solution.py:509
  40.4 5.9 %collective-permute-start.3 = (f32[1,32,256]{2,1,0:T(8,128)S(1)}, f32[1,32,256]{2,1,0:T(8,128)S(1)}, u32[]{:S(2)}, u32[]{:S(2)}) collective-permute-start(f32[1,32,256]{2,1,0:T(8,128)S(1)} %get-tuple-element.26), channel_id=1, source_target_pairs={{0,2},{2,0},{1,3},{3,1},{4,6},{6,4},{5,7},{7,5},{8,10},{10,8},{9,1... | collective-permute-start | bytes 98312 | tf_op jit(solution)/shard_map/ppermute | solution.py:510
  46.3 3.1 %collective-permute-start.4 = (f32[1,32,256]{2,1,0:T(8,128)S(1)}, f32[1,32,256]{2,1,0:T(8,128)S(1)}, u32[]{:S(2)}, u32[]{:S(2)}) collective-permute-start(f32[1,32,256]{2,1,0:T(8,128)S(1)} %add.42), channel_id=1, source_target_pairs={{0,8},{16,24},{8,0},{24,16},{1,9},{17,25},{9,1},{25,17},{2,10},{18... | collective-permute-start | bytes 98312 | tf_op jit(solution)/shard_map/ppermute | solution.py:494
  49.4 4.0 %collective-permute-start.5 = (f32[1,32,256]{2,1,0:T(8,128)S(1)}, f32[1,32,256]{2,1,0:T(8,128)S(1)}, u32[]{:S(2)}, u32[]{:S(2)}) collective-permute-start(f32[1,32,256]{2,1,0:T(8,128)S(1)} %add.43), channel_id=1, source_target_pairs={{0,24},{8,16},{24,0},{16,8},{1,25},{9,17},{25,1},{17,9},{2,26},{10... | collective-permute-start | bytes 98312 | tf_op jit(solution)/shard_map/ppermute | solution.py:494
  53.3 3.1 %collective-permute-start.6 = (f32[1,32,256]{2,1,0:T(8,128)S(1)}, f32[1,32,256]{2,1,0:T(8,128)S(1)}, u32[]{:S(2)}, u32[]{:S(2)}) collective-permute-start(f32[1,32,256]{2,1,0:T(8,128)S(1)} %add.44), channel_id=1, source_target_pairs={{0,32},{64,96},{128,160},{192,224},{32,0},{96,64},{160,128},{224,1... | collective-permute-start | bytes 98312 | tf_op jit(solution)/shard_map/ppermute | solution.py:494
  56.4 3.7 %collective-permute-start.7 = (f32[1,32,256]{2,1,0:T(8,128)S(1)}, f32[1,32,256]{2,1,0:T(8,128)S(1)}, u32[]{:S(2)}, u32[]{:S(2)}) collective-permute-start(f32[1,32,256]{2,1,0:T(8,128)S(1)} %add.45), channel_id=1, source_target_pairs={{0,64},{32,96},{128,192},{160,224},{64,0},{96,32},{192,128},{224,1... | collective-permute-start | bytes 98312 | tf_op jit(solution)/shard_map/ppermute | solution.py:494
  60.1 5.8 %collective-permute-start.8 = (f32[1,32,256]{2,1,0:T(8,128)S(1)}, f32[1,32,256]{2,1,0:T(8,128)S(1)}, u32[]{:S(2)}, u32[]{:S(2)}) collective-permute-start(f32[1,32,256]{2,1,0:T(8,128)S(1)} %add.46), channel_id=1, source_target_pairs={{0,224},{32,192},{64,160},{96,128},{224,0},{192,32},{160,64},{128,... | collective-permute-start | bytes 98312 | tf_op jit(solution)/shard_map/ppermute | solution.py:494
  73.0 3.5 %collective-permute-start.10 = (f32[1,32,256]{2,1,0:T(8,128)S(1)}, f32[1,32,256]{2,1,0:T(8,128)S(1)}, u32[]{:S(2)}, u32[]{:S(2)}) collective-permute-start(f32[1,32,256]{2,1,0:T(8,128)S(1)} %get-tuple-element.31), channel_id=1, source_target_pairs={{0,2},{2,0},{1,3},{3,1},{4,6},{6,4},{5,7},{7,5},{8,10},{10,8},{9,1... | collective-permute-start | bytes 98312 | tf_op jit(solution)/shard_map/ppermute | solution.py:510
  76.5 4.3 %collective-permute-start.11 = (f32[1,32,256]{2,1,0:T(8,128)S(1)}, f32[1,32,256]{2,1,0:T(8,128)S(1)}, u32[]{:S(2)}, u32[]{:S(2)}) collective-permute-start(f32[1,32,256]{2,1,0:T(8,128)S(1)} %add.48), channel_id=1, source_target_pairs={{0,8},{16,24},{8,0},{24,16},{1,9},{17,25},{9,1},{25,17},{2,10},{18... | collective-permute-start | bytes 98312 | tf_op jit(solution)/shard_map/ppermute | solution.py:494
  78.1 4.9 %collective-permute-start.18 = (f32[1,32,256]{2,1,0:T(8,128)S(1)}, f32[1,32,256]{2,1,0:T(8,128)S(1)}, u32[]{:S(2)}, u32[]{:S(2)}) collective-permute-start(f32[1,32,256]{2,1,0:T(8,128)S(1)} %add.47), channel_id=1, source_target_pairs={{0,4},{4,0},{1,5},{5,1},{2,6},{6,2},{3,7},{7,3},{8,12},{12,8},{9,1... | collective-permute-start | bytes 98312 | tf_op jit(solution)/shard_map/ppermute | solution.py:494
  80.8 5.1 %collective-permute-start.12 = (f32[1,32,256]{2,1,0:T(8,128)S(1)}, f32[1,32,256]{2,1,0:T(8,128)S(1)}, u32[]{:S(2)}, u32[]{:S(2)}) collective-permute-start(f32[1,32,256]{2,1,0:T(8,128)S(1)} %add.49), channel_id=1, source_target_pairs={{0,24},{8,16},{24,0},{16,8},{1,25},{9,17},{25,1},{17,9},{2,26},{10... | collective-permute-start | bytes 98312 | tf_op jit(solution)/shard_map/ppermute | solution.py:494
  84.7 13.5 %collective-permute-start.19 = (f32[72,256]{1,0:T(8,128)S(1)}, f32[72,256]{1,0:T(8,128)S(1)}, u32[]{:S(2)}, u32[]{:S(2)}) collective-permute-start(f32[72,256]{1,0:T(8,128)S(1)} %factor.3.full_ref.refs_3_), channel_id=1, source_target_pairs={{0,2},{2,0},{1,3},{3,1},{4,6},{6,4},{5,7},{7,5},{8,10},{10,8},{9,1... | collective-permute-start | bytes 221192 | tf_op jit(solution)/shard_map/ppermute | solution.py:510
  86.0 3.8 %collective-permute-start.13 = (f32[1,32,256]{2,1,0:T(8,128)S(1)}, f32[1,32,256]{2,1,0:T(8,128)S(1)}, u32[]{:S(2)}, u32[]{:S(2)}) collective-permute-start(f32[1,32,256]{2,1,0:T(8,128)S(1)} %add.50), channel_id=1, source_target_pairs={{0,32},{64,96},{128,160},{192,224},{32,0},{96,64},{160,128},{224,1... | collective-permute-start | bytes 98312 | tf_op jit(solution)/shard_map/ppermute | solution.py:494
  89.8 5.1 %collective-permute-start.14 = (f32[1,32,256]{2,1,0:T(8,128)S(1)}, f32[1,32,256]{2,1,0:T(8,128)S(1)}, u32[]{:S(2)}, u32[]{:S(2)}) collective-permute-start(f32[1,32,256]{2,1,0:T(8,128)S(1)} %add.51), channel_id=1, source_target_pairs={{0,64},{32,96},{128,192},{160,224},{64,0},{96,32},{192,128},{224,1... | collective-permute-start | bytes 98312 | tf_op jit(solution)/shard_map/ppermute | solution.py:494
  95.0 5.3 %collective-permute-start.15 = (f32[1,32,256]{2,1,0:T(8,128)S(1)}, f32[1,32,256]{2,1,0:T(8,128)S(1)}, u32[]{:S(2)}, u32[]{:S(2)}) collective-permute-start(f32[1,32,256]{2,1,0:T(8,128)S(1)} %add.52), channel_id=1, source_target_pairs={{0,224},{32,192},{64,160},{96,128},{224,0},{192,32},{160,64},{128,... | collective-permute-start | bytes 98312 | tf_op jit(solution)/shard_map/ppermute | solution.py:494
  100.3 4.8 %collective-permute-start.16 = (f32[1,32,256]{2,1,0:T(8,128)S(1)}, f32[1,32,256]{2,1,0:T(8,128)S(1)}, u32[]{:S(2)}, u32[]{:S(2)}) collective-permute-start(f32[1,32,256]{2,1,0:T(8,128)S(1)} %add.53), channel_id=1, source_target_pairs={{0,4},{4,0},{1,5},{5,1},{2,6},{6,2},{3,7},{7,3},{8,12},{12,8},{9,1... | collective-permute-start | bytes 98312 | tf_op jit(solution)/shard_map/ppermute | solution.py:494
  106.8 7.6 %collective-permute-start.17 = (f32[72,256]{1,0:T(8,128)S(1)}, f32[72,256]{1,0:T(8,128)S(1)}, u32[]{:S(2)}, u32[]{:S(2)}) collective-permute-start(f32[72,256]{1,0:T(8,128)S(1)} %factor.2.full_ref.refs_5_), channel_id=1, source_target_pairs={{0,2},{2,0},{1,3},{3,1},{4,6},{6,4},{5,7},{7,5},{8,10},{10,8},{9,1... | collective-permute-start | bytes 221192 | tf_op jit(solution)/shard_map/ppermute | solution.py:510
